TPU v7x, 512 devices: a whole 4x8x8 slice. The times are simulated.
512 devices in a mesh: dp: 32 (over z_hi, y), tensor: 16 (over x, z_lo, core).
Axes of the slice: x: 4, y: 8, z: 8 (z_hi: 4, z_lo: 2; z = z_hi * 2 + z_lo), core: 2. Of those that a mesh axis runs over, the one named last changes fastest.
Arguments:
- residual: bfloat16 [2048, 8192], P('dp', 'tensor'), may hold values from -120 to 120, as said below
- attention: bfloat16 [2048, 8192], P('dp', 'tensor'), may hold values from -18 to 18
- out_proj: bfloat16 [8192, 8192], P('tensor', 'dp'), may hold values from -0.0625 to 0.0625
- norm_gain: float32 [8192], P('tensor'), may hold values from 0.1 to 1.9
- index_draws: bfloat16 [2048, 64, 8], P('dp', 'tensor'), may hold values from -9 to 9, as said below
- labels: int32 [2048, 25], P('dp'), may hold values 0 or 1
- w_first: bfloat16 [8192, 1024], P('tensor'), may hold values from -0.0625 to 0.0625
- w_index: bfloat16 [8, 1024], replicated, may hold values from -2 to 2
- bias_first: float32 [1024], replicated, may hold values from -4 to 4
- w_hidden: bfloat16 [1024, 1024], replicated, may hold values from -0.1875 to 0.1875
- bias_hidden: float32 [1024], replicated, may hold values from -4 to 4
- w_output: bfloat16 [1024, 200], replicated, may hold values from -0.1875 to 0.1875
Outputs:
- grad_first: float32 [8192, 1024], P('tensor')
- grad_hidden: float32 [1024, 1024], P('tensor', 'dp')
- grad_output: float32 [1024, 200], P('tensor')
Inputs may be any that keep to these rules, and one draw needn't show every extreme that they name: `residual`: residual entries; notes and features have unlike scales. `index_draws`: index sample entries.
All inputs are finite; a program needn't handle non-finite values. No bound on the sum of `labels` on one device may be relied on, other than what follows from the above.
Results may differ from a plain program's by a relative error of at most 0.022.
Values may be sent and summed in bfloat16 or wider, within the bound.
No kernel may reach another device: no remote copies, remote signals or barrier semaphores. Data moves between devices by JAX's collectives and lax.ppermute only.
A program may use at most 64 MiB of HBM per device.

v0:
```python
import jax
import jax.numpy as jnp
from jax import lax
from jax.sharding import PartitionSpec as P

NORM_EPS = 1e-05


def swish(values):
    return values * jax.nn.sigmoid(values)


def swish_slope(values):
    sig = jax.nn.sigmoid(values)
    return sig * (1.0 + values * (1.0 - sig))


def contract_rows(left, right):
    return lax.dot_general(
        left, right, (((0,), (0,)), ((), ())), preferred_element_type=jnp.float32
    )


def contract_cols(left, right):
    return lax.dot_general(
        left, right, (((1,), (1,)), ((), ())), preferred_element_type=jnp.float32
    )


def shards(
    residual,
    attention,
    out_proj,
    norm_gain,
    index_draws,
    labels,
    w_first,
    w_index,
    bias_first,
    w_hidden,
    bias_hidden,
    w_output,
):
    rows = residual.shape[0]
    width = out_proj.shape[0] * lax.axis_size("tensor")
    partial_value = jnp.dot(
        attention,
        lax.all_gather(out_proj, "dp", axis=1, tiled=True),
        preferred_element_type=jnp.float32,
    )
    branch = lax.psum_scatter(
        partial_value.astype(jnp.bfloat16), "tensor", scatter_dimension=1, tiled=True
    ).astype(jnp.float32)
    state = residual.astype(jnp.float32) + branch
    square_sum = lax.psum(jnp.sum(state * state, axis=1), "tensor")
    scale = lax.rsqrt(square_sum / width + NORM_EPS)
    features = (state * scale[:, None] * norm_gain).astype(jnp.bfloat16)
    first_pre = lax.psum(jnp.dot(features, w_first, preferred_element_type=jnp.float32), "tensor")
    local_samples = index_draws.shape[1]
    index_width = index_draws.shape[2]
    hidden_units = w_hidden.shape[0]
    classes = labels.shape[1]
    pair_count = rows * local_samples
    total_samples = local_samples * lax.axis_size("tensor")
    draws = index_draws.reshape(pair_count, index_width)
    index_term = jnp.dot(draws, w_index, preferred_element_type=jnp.float32).reshape(
        rows, local_samples, hidden_units
    )
    pre_first = (first_pre[:, None, :] + index_term + bias_first).reshape(pair_count, hidden_units)
    act_first = swish(pre_first).astype(jnp.bfloat16)
    pre_second = jnp.dot(act_first, w_hidden, preferred_element_type=jnp.float32) + bias_hidden
    act_second = swish(pre_second).astype(jnp.bfloat16)
    readout = jnp.dot(act_second, w_output, preferred_element_type=jnp.float32).reshape(
        pair_count, classes, index_width
    )
    index_float = draws.astype(jnp.float32)
    logits = jnp.sum(readout * index_float[:, None, :], axis=2)
    targets = (
        jnp.broadcast_to(labels[:, None, :], (rows, local_samples, classes))
        .reshape(pair_count, classes)
        .astype(jnp.float32)
    )
    logit_grad = (jax.nn.sigmoid(logits) - targets) / total_samples
    out_cot = (
        (logit_grad[:, :, None] * index_float[:, None, :])
        .reshape(pair_count, classes * index_width)
        .astype(jnp.bfloat16)
    )
    output_rows = lax.psum_scatter(
        contract_rows(act_second, out_cot).astype(jnp.bfloat16),
        "tensor",
        scatter_dimension=0,
        tiled=True,
    ).astype(jnp.float32)
    grad_output = lax.psum(output_rows, "dp")
    second_grad = (contract_cols(out_cot, w_output) * swish_slope(pre_second)).astype(jnp.bfloat16)
    hidden_rows = lax.psum_scatter(
        contract_rows(act_first, second_grad).astype(jnp.bfloat16),
        "tensor",
        scatter_dimension=0,
        tiled=True,
    ).astype(jnp.float32)
    grad_hidden = lax.psum_scatter(hidden_rows, "dp", scatter_dimension=1, tiled=True)
    first_grad = (contract_cols(second_grad, w_hidden) * swish_slope(pre_first)).astype(
        jnp.bfloat16
    )
    row_sum = jnp.sum(
        first_grad.reshape(rows, local_samples, hidden_units), axis=1, dtype=jnp.float32
    )
    row_grad = lax.psum(row_sum, "tensor").astype(jnp.bfloat16)
    first_term = contract_rows(features, row_grad).astype(jnp.bfloat16).astype(jnp.float32)
    grad_first = lax.psum(first_term, "dp")
    return (grad_first, grad_hidden, grad_output)


def solution(mesh):
    placed = (
        P("dp", "tensor"),
        P("dp", "tensor"),
        P("tensor", "dp"),
        P("tensor"),
        P("dp", "tensor", None),
        P("dp", None),
        P("tensor", None),
        P(),
        P(),
        P(),
        P(),
        P(),
    )
    return jax.shard_map(
        shards,
        mesh=mesh,
        in_specs=placed,
        out_specs=(P("tensor", None), P("tensor", "dp"), P("tensor", None)),
        check_vma=False,
    )
```

profile of v0, /device:TPU:6, one launch (start us, length us, event | category | flops | bytes accessed | tf_op | source)
XLA Modules:
  0.0 1102.1 jit_solution(4723644746815220655)
XLA Ops:
  7.2 0.0 copy-start
  7.2 0.0 all-gather.2.cloned.1.call-start
  7.2 0.7 all-gather.2.cloned.1.call-update
  7.9 0.0 copy-start.3
  7.9 0.0 copy-start.1
  7.9 0.0 copy-start.9
  7.9 0.0 reduce-scatter.7.cloned.1.call-start
  8.0 159.3 %all-gather.2.cloned.1.call-done = bf16[512,8192]{1,0:T(8,128)(2,1)} async-done(((bf16[512,256]{1,0:T(8,128)(2,1)}), bf16[512,8192]{1,0:T(8,128)(2,1)}) %all-gather.2.cloned.1.call-update) | async-done | bytes 8388624 | tf_op jit(solution)/shard_map/all_gather | solution.py:48
  167.2 6.0 convolution_convert_fusion
  173.2 0.0 reduce-scatter.7.cloned.1.call-update
  173.2 0.0 all-reduce.4.cloned.1.call-start
  173.3 55.0 %reduce-scatter.7.cloned.1.call-done = bf16[64,512]{1,0:T(8,128)(2,1)} async-done(((bf16[64,8192]{1,0:T(8,128)(2,1)}), bf16[64,512]{1,0:T(8,128)(2,1)}) %reduce-scatter.7.cloned.1.call-update) | async-done | bytes 65552 | tf_op jit(solution)/shard_map/reduce_scatter | solution.py:51
  228.3 0.0 copy-done.3
  228.3 1.0 multiply_reduce_fusion
  229.3 27.2 %psum.35 = f32[64]{0:T(128)S(1)} all-reduce(f32[64]{0:T(128)S(1)} %multiply_reduce_fusion), channel_id=1, replica_groups=mesh['dp'=32,'tensor'=16] {'tensor'}, use_global_device_ids=true, to_apply=%region_2.0 | all-reduce | flops 64 | bytes 512 | tf_op jit(solution)/shard_map/psum | solution.py:55
  256.5 0.0 copy-done.1
  256.5 0.0 copy-done.9
  256.5 1.9 fusion.16
  258.4 0.0 all-reduce.4.cloned.1.call-update
  258.4 0.0 reduce-scatter.9.cloned.1.call-start
  258.5 0.0 copy-done.7
  258.5 0.1 copy.25
  258.6 0.1 copy.26
  258.7 0.0 copy-done.6
  258.7 0.1 copy.23
  258.9 0.1 copy.24
  258.9 127.6 %all-reduce.4.cloned.1.call-done = f32[64,1024]{1,0:T(8,128)} async-done(((f32[64,1024]{1,0:T(8,128)}), f32[64,1024]{1,0:T(8,128)}) %all-reduce.4.cloned.1.call-update) | async-done | bytes 262160 | tf_op jit(solution)/shard_map/psum | solution.py:58
  386.5 0.0 copy-done.8
  386.5 0.0 copy-done.10
  386.5 1.3 fusion.1
  387.8 0.0 copy-start.12
  387.8 0.7 copy.22
  388.5 1.3 reshape.52
  389.8 0.0 copy-done
  389.8 0.0 copy-done.12
  389.8 2.1 multiply_convert_fusion
  392.0 0.0 copy-start.5
  392.0 0.0 copy-done.11
  392.0 0.3 fusion.6
  392.4 0.4 copy-done.5
  392.8 0.5 fusion.2
  393.3 0.8 copy-done.13
  394.1 0.0 copy-done.2
  394.1 2.2 convolution_convert_fusion.1
  396.3 0.0 reduce-scatter.9.cloned.1.call-update
  396.3 0.0 reduce-scatter.11.cloned.1.call-start
  396.3 2.2 convolution_convert_fusion.3
  398.5 0.0 reduce-scatter.11.cloned.1.call-update
  398.5 0.0 all-reduce.6.cloned.1.call-start
  398.6 2.9 fusion.4
  401.5 1.6 reshape.55
  403.0 0.6 reduce_sum.29
  403.7 57.1 %all-reduce.7 = bf16[64,1024]{1,0:T(8,128)(2,1)S(1)} all-reduce(f32[64,1024]{1,0:T(8,128)S(1)} %reduce_sum.29), channel_id=1, replica_groups=mesh['dp'=32,'tensor'=16] {'tensor'}, use_global_device_ids=true, to_apply=%region_6.0 | all-reduce | flops 65536 | bytes 393216 | tf_op jit(solution)/shard_map/psum | solution.py:110
  460.8 1.9 fusion
  462.6 0.0 all-reduce.6.cloned.1.call-update
  462.7 0.0 reduce-scatter.13.cloned.1.call-start
  462.7 2.2 reduce-scatter.9.cloned.1.call-done
  464.9 1.8 copy.28
  466.8 0.0 reduce-scatter.13.cloned.1.call-update
  466.8 65.9 %reduce-scatter.11.cloned.1.call-done = bf16[64,200]{1,0:T(8,128)(2,1)} async-done(((bf16[1024,200]{1,0:T(8,128)(2,1)}), bf16[64,200]{1,0:T(8,128)(2,1)}) %reduce-scatter.11.cloned.1.call-update) | async-done | bytes 25616 | tf_op jit(solution)/shard_map/reduce_scatter | solution.py:89
  532.7 159.3 %psum.39 = f32[64,200]{1,0:T(8,128)} all-reduce(bf16[64,200]{1,0:T(8,128)(2,1)} %reduce-scatter.11.cloned.1.call-done), channel_id=1, replica_groups=mesh['dp'=32,'tensor'=16] {'dp'}, use_global_device_ids=true, to_apply=%region_11.0 | all-reduce | flops 12800 | bytes 76800 | tf_op jit(solution)/shard_map/psum | solution.py:95
  692.0 174.6 %all-reduce.6.cloned.1.call-done = f32[512,1024]{1,0:T(8,128)} async-done(((f32[512,1024]{1,0:T(8,128)}), f32[512,1024]{1,0:T(8,128)}) %all-reduce.6.cloned.1.call-update) | async-done | bytes 2097168 | tf_op jit(solution)/shard_map/psum | solution.py:112
  866.5 225.5 %reduce-scatter.13.cloned.1.call-done = f32[32,64]{1,0:T(8,128)} async-done(((f32[1024,64]{1,0:T(8,128)}), f32[32,64]{1,0:T(8,128)}) %reduce-scatter.13.cloned.1.call-update) | async-done | bytes 8208
  1092.1 3.2 copy.34
  (13 shorter events, 0.1 us)
Async XLA Ops:
  7.2 382.7 %copy-start = (bf16[1024,1024]{1,0:T(8,128)(2,1)S(1)}, bf16[1024,1024]{1,0:T(8,128)(2,1)}, u32[]{:S(2)}) copy-start(bf16[1024,1024]{1,0:T(8,128)(2,1)} %param.21) | copy-start | bytes 6291460
  7.2 160.1 %all-gather.2.cloned.1.call-start = ((), (), s32[]{:S(2)}) async-start(), calls=%async_computation.4 | async-start | bytes 8650752 | tf_op jit(solution)/shard_map/all_gather | solution.py:48
  7.9 220.4 %copy-start.3 = (bf16[64,512]{1,0:T(8,128)(2,1)S(1)}, bf16[64,512]{1,0:T(8,128)(2,1)}, u32[]{:S(2)}) copy-start(bf16[64,512]{1,0:T(8,128)(2,1)} %param.12) | copy-start | bytes 196612
  7.9 248.6 %copy-start.1 = (bf16[512,1024]{1,0:T(8,128)(2,1)S(1)}, bf16[512,1024]{1,0:T(8,128)(2,1)}, u32[]{:S(2)}) copy-start(bf16[512,1024]{1,0:T(8,128)(2,1)} %param.18) | copy-start | bytes 3145732
  7.9 248.6 %copy-start.9 = (f32[512]{0:T(512)S(1)}, f32[512]{0:T(512)}, u32[]{:S(2)}) copy-start(f32[512]{0:T(512)} %param.15) | copy-start | bytes 6148
  7.9 220.4 %reduce-scatter.7.cloned.1.call-start = ((), (), s32[]{:S(2)}) async-start(), calls=%async_computation.5 | async-start | bytes 1114112 | tf_op jit(solution)/shard_map/reduce_scatter | solution.py:51
  173.2 85.3 %copy-start.7 = (s32[64,25]{0,1:T(8,128)S(1)}, s32[64,25]{0,1:T(8,128)}, u32[]{:S(2)}) copy-start(s32[64,25]{0,1:T(8,128)} %param.17) | copy-start | bytes 19204
  173.2 85.5 %copy-start.6 = (bf16[64,4,8]{0,2,1:T(8,128)(2,1)S(1)}, bf16[64,4,8]{0,2,1:T(8,128)(2,1)}, u32[]{:S(2)}) copy-start(bf16[64,4,8]{0,2,1:T(8,128)(2,1)} %param.16) | copy-start | bytes 12292
  173.2 213.3 %copy-start.8 = (bf16[8,1024]{1,0:T(8,128)(2,1)S(1)}, bf16[8,1024]{1,0:T(8,128)(2,1)}, u32[]{:S(2)}) copy-start(bf16[8,1024]{1,0:T(8,128)(2,1)} %param.19) | copy-start | bytes 49156
  173.2 213.3 %copy-start.10 = (f32[1024]{0:T(1024)S(1)}, f32[1024]{0:T(1024)}, u32[]{:S(2)}) copy-start(f32[1024]{0:T(1024)} %param.20) | copy-start | bytes 12292
  173.2 213.3 %all-reduce.4.cloned.1.call-start = ((), (), s32[]{:S(2)}) async-start(), calls=%async_computation.6 | async-start | bytes 524288 | tf_op jit(solution)/shard_map/psum | solution.py:58
  258.4 206.5 %reduce-scatter.9.cloned.1.call-start = ((), (), s32[]{:S(2)}) async-start(), calls=%async_computation.8 | async-start | bytes 2228224 | tf_op jit(solution)/shard_map/reduce_scatter | solution.py:97
  387.8 2.0 copy-start.12
  389.8 2.1 copy-start.11
  392.0 0.8 copy-start.5
  392.8 1.3 copy-start.2
  393.3 0.8 copy-start.13
  396.3 136.4 %reduce-scatter.11.cloned.1.call-start = ((), (), s32[]{:S(2)}) async-start(), calls=%async_computation.9 | async-start | bytes 557056 | tf_op jit(solution)/shard_map/reduce_scatter | solution.py:89
  398.5 468.0 %all-reduce.6.cloned.1.call-start = ((), (), s32[]{:S(2)}) async-start(), calls=%async_computation.7 | async-start | bytes 4194304 | tf_op jit(solution)/shard_map/psum | solution.py:112
  401.5 59.3 %copy-start.4 = (bf16[64,512]{1,0:T(8,128)(2,1)S(1)}, bf16[64,512]{1,0:T(8,128)(2,1)}, u32[]{:S(2)}) copy-start(bf16[64,512]{1,0:T(8,128)(2,1)} %reduce-scatter.7.cloned.1.call-done) | copy-start | bytes 196612
  462.7 629.4 %reduce-scatter.13.cloned.1.call-start = ((), (), s32[]{:S(2)}) async-start(), calls=%async_computation.10 | async-start | bytes 540672
Sparse Core Ops, SparseCore 0:
  11.1 156.1 all-gather.1
  173.4 54.9 reduce-scatter.6
  258.6 127.8 all-reduce.3
  396.4 68.4 reduce-scatter.8
  467.6 65.0 reduce-scatter.10
  536.3 330.1 all-reduce.5
  871.5 220.4 reduce-scatter.12
where the time goes:
time: 1100 us
  waiting for transfers between devices  811 us (74%)
  blocking collectives  244 us (22%)
  matrix products  21.2 us (2%)
  between operations  14.3 us (1%)
    unnamed x8, waiting for transfers between devices  226 us
    psum x1, waiting for transfers between devices, shards(): grad_first = lax.psum(first_term, 'dp')  175 us
    psum x1, blocking collectives, shards(): grad_output = lax.psum(output_rows, 'dp')  159 us
    all_gather x1, waiting for transfers between devices, shards(): lax.all_gather(out_proj, 'dp', axis=1, tiled=True)  159 us
    psum x1, waiting for transfers between devices, shards(): lax.psum(jnp.dot(features, w_first, preferred_element_type=jnp.float32),...  128 us
    reduce_scatter x1, waiting for transfers between devices, shards(): lax.psum_scatter(contract_rows(act_second, out_cot).astype(jnp.bfloat16),...  65.9 us
    psum x1, blocking collectives, shards(): row_grad = lax.psum(row_sum, 'tensor').astype(jnp.bfloat16)  57.1 us
    reduce_scatter x1, waiting for transfers between devices, shards(): lax.psum_scatter(partial_value.astype(jnp.bfloat16), 'tensor', scatter_di...  55 us
  transfers between devices with their start and end apart: 7, of which 7 were waited for; matrix products, arithmetic and copies ran while one was open for 1% of the time, Pallas kernels for 0%

commit v1 on v0

v1 whole, which is shorter than its diff:
```python
import jax
import jax.numpy as jnp
from jax import lax
from jax.sharding import Mesh, PartitionSpec as P

NORM_EPS = 1e-05
bf16, f32 = jnp.bfloat16, jnp.float32
DP = ("zh", "y")
TENSOR = ("x", "zl", "c")
PARTS = {"zh": 4, "y": 8, "x": 4, "zl": 2, "c": 2}


def swish_slope(values, sig):
    return sig * (1.0 + values * (1.0 - sig))


def contract(left, right, left_dim, right_dim):
    return lax.dot_general(
        left, right, (((left_dim,), (right_dim,)), ((), ())), preferred_element_type=f32
    )


def exchange(blocks, axes):
    return lax.all_to_all(blocks, axes, 0, 0, tiled=True)


def spread(block, axes, count):
    return exchange(jnp.broadcast_to(block[None], (count,) + block.shape), axes)


def shards(
    residual,
    attention,
    out_proj,
    norm_gain,
    index_draws,
    labels,
    w_first,
    w_index,
    bias_first,
    w_hidden,
    bias_hidden,
    w_output,
):
    rows, width = residual.shape
    n_zh, n_y, n_t = PARTS["zh"], PARTS["y"], 16
    y, zl, c = lax.axis_index("y"), lax.axis_index("zl"), lax.axis_index("c")
    tensor = lax.axis_index(TENSOR)
    cols = out_proj.shape[1]
    quarter = cols // 4
    own = rows // n_t
    samples = index_draws.shape[1] * n_t
    idx = index_draws.shape[2]
    hidden = w_hidden.shape[0]
    classes = labels.shape[1]
    reads = classes * idx

    draws = exchange(index_draws.reshape(n_t, own, -1), TENSOR)
    draws = draws.reshape(n_t, own, samples // n_t, idx).transpose(1, 0, 2, 3)
    draws = draws.reshape(own * samples, idx)
    index_term = jnp.dot(draws, w_index, preferred_element_type=f32) + bias_first
    tile = (jnp.arange(reads)[None, :] % idx == jnp.arange(idx)[:, None]).astype(bf16)
    draws_rep = jnp.dot(draws, tile, preferred_element_type=f32)
    own_labels = lax.dynamic_slice_in_dim(labels, tensor * own, own, 0).astype(f32)
    targets = jnp.broadcast_to(own_labels[:, :, None], (own, classes, idx)).reshape(own, 1, reads)

    att = spread(attention, "y", n_y).reshape(n_y * rows, width)
    proj = spread(out_proj, "zh", n_zh)
    part = contract(proj, att, 1, 1).astype(bf16)
    part = part.reshape(n_zh * 2, 2, quarter, n_y * rows)
    mine = lax.dynamic_index_in_dim(part, c, 1, keepdims=False)
    other = lax.dynamic_index_in_dim(part, 1 - c, 1, keepdims=False)
    swapped = lax.ppermute(other, "c", [(0, 1), (1, 0)])
    pair = (mine.astype(f32) + swapped.astype(f32)).astype(bf16)
    branch = jnp.sum(exchange(pair, ("x", "zl")).astype(f32), axis=0).astype(bf16)
    branch = branch.reshape(quarter, n_y, rows).transpose(1, 0, 2)
    slot = (jnp.arange(4) == y // 2)[None, :, None, None]
    branch = jnp.where(slot, branch[:, None], jnp.zeros((), bf16))
    branch = exchange(branch.reshape(n_y * 4, quarter, rows), ("y", "zl", "c"))
    branch = branch.reshape(n_y, 4 * quarter, rows)
    branch = lax.dynamic_slice_in_dim(branch, 2 * (2 * zl + c), 2, 0).reshape(width, rows)

    state = residual.astype(f32).T + branch.astype(f32)
    square_sum = jnp.sum(state * state, axis=0)
    gained = (state * norm_gain[:, None]).astype(bf16)
    gained_all = lax.all_gather(gained, "zh", axis=0)
    first = contract(gained, w_first, 0, 0)
    high = square_sum.astype(bf16)
    low = (square_sum - high.astype(f32)).astype(bf16)
    extra = jnp.concatenate(
        [high[:, None], low[:, None], jnp.zeros((rows, 126), bf16)], axis=1
    )
    first = jnp.concatenate([first.astype(bf16), extra], axis=1).reshape(n_t, own, hidden + 128)
    first = jnp.sum(exchange(first, TENSOR).astype(f32), axis=0)
    square_sum = first[:, hidden] + first[:, hidden + 1]
    scale = lax.rsqrt(square_sum / (width * n_t) + NORM_EPS)
    first_pre = first[:, :hidden] * scale[:, None]

    pairs = own * samples
    pre_first = (
        first_pre[:, None, :] + index_term.reshape(own, samples, hidden)
    ).reshape(pairs, hidden)
    sig_first = jax.nn.sigmoid(pre_first)
    act_first = (pre_first * sig_first).astype(bf16)
    pre_second = jnp.dot(act_first, w_hidden, preferred_element_type=f32) + bias_hidden
    sig_second = jax.nn.sigmoid(pre_second)
    act_second = (pre_second * sig_second).astype(bf16)
    readout = jnp.dot(act_second, w_output, preferred_element_type=f32)
    same = (jnp.arange(reads)[:, None] // idx == jnp.arange(reads)[None, :] // idx).astype(f32)
    logits = jnp.dot(readout * draws_rep, same, precision=lax.Precision.HIGHEST)
    logit_grad = jax.nn.sigmoid(logits).reshape(own, samples, reads) - targets
    out_cot = (logit_grad.reshape(pairs, reads) / samples * draws_rep).astype(bf16)
    output_part = contract(act_second, out_cot, 0, 0).astype(bf16)
    second_grad = (
        contract(out_cot, w_output, 1, 1) * swish_slope(pre_second, sig_second)
    ).astype(bf16)
    hidden_part = contract(act_first, second_grad, 0, 0).astype(bf16)
    first_grad = (
        contract(second_grad, w_hidden, 1, 1) * swish_slope(pre_first, sig_first)
    ).astype(bf16)
    row_sum = jnp.sum(first_grad.reshape(own, samples, hidden), axis=1, dtype=f32)
    row_grad = (row_sum * scale[:, None]).astype(bf16)

    row_blocks = row_grad.reshape(own, n_zh, cols).transpose(1, 0, 2)
    row_blocks = jnp.broadcast_to(row_blocks[:, None], (n_zh, n_t, own, cols))
    row_blocks = exchange(row_blocks.reshape(n_zh * n_t, own, cols), ("zh",) + TENSOR)
    row_blocks = row_blocks.reshape(n_zh * rows, cols)

    pad = jnp.zeros((hidden, 256 - reads), bf16)
    weights = jnp.concatenate([hidden_part, output_part, pad], axis=1)
    weights = weights.reshape(n_t // 2, 2, hidden // n_t, hidden + 256)
    mine = lax.dynamic_index_in_dim(weights, c, 1, keepdims=False)
    other = lax.dynamic_index_in_dim(weights, 1 - c, 1, keepdims=False)
    swapped = lax.ppermute(other, "c", [(0, 1), (1, 0)])
    weights = (mine.astype(f32) + swapped.astype(f32)).astype(bf16)
    weights = jnp.sum(exchange(weights, ("x", "zl")).astype(f32), axis=0).astype(bf16)
    hidden_rows = hidden // n_t
    output_rows = weights[:, hidden:].reshape(n_y, hidden_rows // n_y, 256)
    hidden_cols = hidden // (n_zh * n_y)
    hidden_blocks = weights[:, :hidden].reshape(hidden_rows, n_zh * n_y, hidden_cols)
    hidden_blocks = hidden_blocks.transpose(1, 0, 2).reshape(n_zh * n_y, 8, 256)

    gained_all = gained_all.transpose(1, 0, 2).reshape(width, n_zh * rows)
    grads = jnp.dot(gained_all, row_blocks, preferred_element_type=f32).astype(bf16)
    grads = jnp.concatenate([grads.reshape(n_y, width // n_y, cols), output_rows], axis=1)
    grads = jnp.sum(exchange(grads, "y").astype(f32), axis=0).astype(bf16)

    grads = jnp.broadcast_to(grads[None], (n_zh * n_y,) + grads.shape)
    grads = exchange(jnp.concatenate([grads, hidden_blocks], axis=1), DP)
    grads = grads.reshape(n_zh, n_y, -1, cols)
    depth = width // n_y
    grad_first = grads[:, :, :depth].astype(f32).transpose(1, 2, 0, 3).reshape(width, hidden)
    grad_output = jnp.sum(grads[:, :, depth : depth + 8].astype(f32), axis=0)
    grad_output = grad_output.reshape(hidden_rows, 256)[:, :reads]
    grad_hidden = jnp.sum(grads[:, :, depth + 8 :].astype(f32), axis=(0, 1))
    grad_hidden = grad_hidden.reshape(hidden_rows, hidden_cols)
    return (grad_first, grad_hidden, grad_output)


def solution(mesh):
    fine = Mesh(mesh.devices.reshape(tuple(PARTS.values())), tuple(PARTS))
    placed = (
        P(DP, TENSOR),
        P(DP, TENSOR),
        P(TENSOR, DP),
        P(TENSOR),
        P(DP, TENSOR, None),
        P(DP, None),
        P(TENSOR, None),
        P(),
        P(),
        P(),
        P(),
        P(),
    )
    return jax.shard_map(
        shards,
        mesh=fine,
        in_specs=placed,
        out_specs=(P(TENSOR, None), P(TENSOR, DP), P(TENSOR, None)),
        check_vma=False,
    )
```

time: 1100 us -> 267 us (0.24)
  waiting for transfers between devices: 811 us -> 77 us
  blocking collectives: 244 us -> 64.6 us
  starting transfers between devices: 0.28 us -> 66.3 us
  local copies, waits for them, and re-layouts: 10.2 us -> 32.1 us
  between operations: 14.3 us -> 1.11 us
  other arithmetic: 1.63 us -> 13.2 us
  matrix products: 21.2 us -> 10.1 us
    psum x2 -> x0, waiting for transfers between devices: 302 us -> none  [the longest x1 175 us: shards(): grad_first = lax.psum(first_term, 'dp')]
    psum x3 -> x0, blocking collectives: 244 us -> none  [the longest x1 159 us: shards(): grad_output = lax.psum(output_rows, 'dp')]
    unnamed x8 -> x0, waiting for transfers between devices: 226 us -> none
    all_gather x1 -> x0, waiting for transfers between devices: 159 us -> none  [shards(): lax.all_gather(out_proj, 'dp', axis=1, tiled=True)]
    reduce_scatter x3 -> x0, waiting for transfers between devices: 123 us -> none  [the longest x1 65.9 us: shards(): lax.psum_scatter(contract_rows(act_second, out_cot).astype(jnp.bfloat16),...]
    all_to_all x0 -> x9, waiting for transfers between devices: none -> 75.1 us  [exchange(): return lax.all_to_all(blocks, axes, 0, 0, tiled=True)]
    all_to_all x0 -> x9, starting transfers between devices: none -> 62.4 us  [exchange(): return lax.all_to_all(blocks, axes, 0, 0, tiled=True)]
    all_to_all x0 -> x1, blocking collectives: none -> 38.6 us  [exchange(): return lax.all_to_all(blocks, axes, 0, 0, tiled=True)]
  transfers between devices with their start and end apart: 7 -> 11, of which waited for: 7 -> 8; matrix products, arithmetic and copies ran while one was open for 1% -> 8% of each run, Pallas kernels for 0% -> 0%
where the time goes in v1:
time: 267 us; the launch traced here: 264 us
  waiting for transfers between devices  77 us (29%)
  starting transfers between devices  66.3 us (25%)
  blocking collectives  64.6 us (24%)
  local copies, waits for them, and re-layouts  32.1 us (12%)
  other arithmetic  13.2 us (5%)
  matrix products  10.1 us (4%)
    all_to_all x9, waiting for transfers between devices, exchange(): return lax.all_to_all(blocks, axes, 0, 0, tiled=True)  75.1 us
    all_to_all x9, starting transfers between devices, exchange(): return lax.all_to_all(blocks, axes, 0, 0, tiled=True)  62.4 us
    all_to_all x1, blocking collectives, exchange(): return lax.all_to_all(blocks, axes, 0, 0, tiled=True)  38.6 us
    all_gather x1, blocking collectives, shards(): gained_all = lax.all_gather(gained, 'zh', axis=0)  26 us
    unnamed x36, local copies, waits for them, and re-layouts  7.45 us
    dot_general x6, matrix products, contract(): lax.dot_general(left, right, (((left_dim,), (right_dim,)), ((), ())), pre...  5.94 us
  transfers between devices with their start and end apart: 11, of which 8 were waited for; matrix products, arithmetic and copies ran while one was open for 8% of the time, Pallas kernels for 0%

profile of v1, /device:TPU:6, one launch (start us, length us, event | category | flops | bytes accessed | tf_op | source)
XLA Modules:
  0.0 264.4 jit_solution(18249313484900942692)
XLA Ops:
  0.6 1.8 broadcast_in_dim.44
  2.5 7.1 %all-to-all-start.1 = ((bf16[8,64,512]{2,1,0:T(8,128)(2,1)}), bf16[8,64,512]{2,1,0:T(8,128)(2,1)S(1)}, u32[]{:S(2)}, u32[]{:S(2)}) async-start(bf16[8,64,512]{2,1,0:T(8,128)(2,1)} %broadcast_in_dim.44), calls=%async_computation.1 | async-start | bytes 1048576 | tf_op jit(solution)/shard_map/all_to_all | solution.py:24
  9.6 1.1 copy.84
  10.7 16.4 %all-to-all-done.1 = bf16[8,64,512]{2,1,0:T(8,128)(2,1)S(1)} async-done(((bf16[8,64,512]{2,1,0:T(8,128)(2,1)}), bf16[8,64,512]{2,1,0:T(8,128)(2,1)S(1)}, u32[]{:S(2)}, u32[]{:S(2)}) %all-to-all-start.1) | async-done | bytes 524320 | tf_op jit(solution)/shard_map/all_to_all | solution.py:24
  27.1 1.2 broadcast_in_dim.43
  28.2 10.3 %all-to-all-start = ((bf16[4,512,256]{1,2,0:T(8,128)(2,1)}), bf16[4,512,256]{1,2,0:T(8,128)(2,1)S(1)}, u32[]{:S(2)}, u32[]{:S(2)}) async-start(bf16[4,512,256]{1,2,0:T(8,128)(2,1)} %broadcast_in_dim.43), calls=%async_computation | async-start | bytes 2097152 | tf_op jit(solution)/shard_map/all_to_all | solution.py:24
  38.5 20.2 %all-to-all-done = bf16[4,512,256]{1,2,0:T(8,128)(2,1)S(1)} async-done(((bf16[4,512,256]{1,2,0:T(8,128)(2,1)}), bf16[4,512,256]{1,2,0:T(8,128)(2,1)S(1)}, u32[]{:S(2)}, u32[]{:S(2)}) %all-to-all-start) | async-done | bytes 1048608 | tf_op jit(solution)/shard_map/all_to_all | solution.py:24
  58.7 1.8 convolution_convert_fusion.1
  60.5 1.0 copy-done.3
  61.5 1.9 collective-permute-start
  63.5 1.9 collective-permute-done
  65.3 2.0 fusion.11
  67.3 13.6 %all-to-all-start.2 = ((bf16[8,64,512]{2,1,0:T(8,128)(2,1)}), bf16[8,64,512]{2,1,0:T(8,128)(2,1)S(1)}, u32[]{:S(2)}, u32[]{:S(2)}) async-start(bf16[8,64,512]{2,1,0:T(8,128)(2,1)} %fusion.11), calls=%async_computation.2 | async-start | bytes 1048576 | tf_op jit(solution)/shard_map/all_to_all | solution.py:24
  81.1 7.9 %all-to-all-done.2 = bf16[8,64,512]{2,1,0:T(8,128)(2,1)S(1)} async-done(((bf16[8,64,512]{2,1,0:T(8,128)(2,1)}), bf16[8,64,512]{2,1,0:T(8,128)(2,1)S(1)}, u32[]{:S(2)}, u32[]{:S(2)}) %all-to-all-start.2) | async-done | bytes 524320 | tf_op jit(solution)/shard_map/all_to_all | solution.py:24
  89.4 1.1 reshape.264
  90.6 4.0 %all-to-all-start.3 = ((bf16[32,2,2048]{2,1,0:T(2,128)(2,1)}), bf16[32,2,2048]{2,1,0:T(2,128)(2,1)S(1)}, u32[]{:S(2)}, u32[]{:S(2)}) async-start(bf16[32,2,2048]{2,1,0:T(2,128)(2,1)} %reshape.264), calls=%async_computation.3 | async-start | bytes 524288 | tf_op jit(solution)/shard_map/all_to_all | solution.py:24
  94.7 0.7 reshape.238
  95.5 11.4 %all-to-all-done.3 = bf16[32,2,2048]{2,1,0:T(2,128)(2,1)S(1)} async-done(((bf16[32,2,2048]{2,1,0:T(2,128)(2,1)}), bf16[32,2,2048]{2,1,0:T(2,128)(2,1)S(1)}, u32[]{:S(2)}, u32[]{:S(2)}) %all-to-all-start.3) | async-done | bytes 262176 | tf_op jit(solution)/shard_map/all_to_all | solution.py:24
  106.9 5.7 %all-to-all-start.5 = ((bf16[16,4,32]{2,1,0:T(4,128)(2,1)}), bf16[16,4,32]{2,1,0:T(4,128)(2,1)S(1)}, u32[]{:S(2)}, u32[]{:S(2)}) async-start(bf16[16,4,32]{2,1,0:T(4,128)(2,1)} %reshape.238), calls=%async_computation.5 | async-start | bytes 32768 | tf_op jit(solution)/shard_map/all_to_all | solution.py:24
  112.7 0.4 reshape.265
  113.0 0.3 copy.86
  113.4 0.3 reshape.236
  113.8 1.0 multiply_reduce_fusion
  115.0 1.6 convolution_convert_fusion.4
  116.9 0.8 concatenate.16
  117.7 5.7 %all-to-all-start.4 = ((bf16[16,4,1152]{2,1,0:T(4,128)(2,1)}), bf16[16,4,1152]{2,1,0:T(4,128)(2,1)S(1)}, u32[]{:S(2)}, u32[]{:S(2)}) async-start(bf16[16,4,1152]{2,1,0:T(4,128)(2,1)} %concatenate.16), calls=%async_computation.4 | async-start | bytes 294912 | tf_op jit(solution)/shard_map/all_to_all | solution.py:24
  124.4 3.5 %all-to-all-done.4 = bf16[16,4,1152]{2,1,0:T(4,128)(2,1)S(1)} async-done(((bf16[16,4,1152]{2,1,0:T(4,128)(2,1)}), bf16[16,4,1152]{2,1,0:T(4,128)(2,1)S(1)}, u32[]{:S(2)}, u32[]{:S(2)}) %all-to-all-start.4) | async-done | bytes 147488 | tf_op jit(solution)/shard_map/all_to_all | solution.py:24
  128.8 0.9 multiply_convert_fusion
  129.6 0.4 copy-done.5
  130.0 0.4 convolution_multiply_fusion.2
  130.4 0.5 fusion.10
  130.9 0.3 convolution_convert_fusion.2
  131.2 0.5 fusion.2
  131.7 0.8 copy-done.12
  132.5 0.8 convolution_convert_fusion
  133.3 2.0 maximum_maximum_fusion
  135.3 4.4 %copy.98 = bf16[1024,1280]{1,0:T(8,128)(2,1)} copy(bf16[1024,1280]{0,1:T(8,128)(2,1)} %maximum_maximum_fusion) | data formatting | bytes 5242880 | tf_op jit(solution)/shard_map/concatenate | solution.py:130
  139.7 2.6 dynamic-slice_bitcast_fusion
  142.3 2.0 collective-permute-start.1
  144.4 1.0 convert_reduce_fusion
  145.5 0.7 broadcast_in_dim.86
  146.1 7.4 %all-to-all-start.6 = ((bf16[64,4,256]{2,1,0:T(4,128)(2,1)}), bf16[64,4,256]{2,1,0:T(4,128)(2,1)}, u32[]{:S(2)}, u32[]{:S(2)}) async-start(bf16[64,4,256]{2,1,0:T(4,128)(2,1)} %bitcast.103), calls=%async_computation.6 | async-start | bytes 262144 | tf_op jit(solution)/shard_map/all_to_all | solution.py:24
  153.6 2.7 %fusion = bf16[8,64,1280]{2,1,0:T(8,128)(2,1)} fusion(bf16[8,64,1280]{2,1,0:T(8,128)(2,1)S(1)} %collective-permute-done.1, bf16[8,2,64,1280]{3,2,1,0:T(8,128)(2,1)} %bitcast.85, s32[]{:T(128)S(6)} %select_n.56), kind=kLoop, calls=%fused_computation.2 | loop fusion | flops 2621440 | bytes 3932164 | tf_op jit(solution)/shard_map/convert_element_type | solution.py:135
  156.2 6.6 %all-to-all-done.6 = bf16[64,4,256]{2,1,0:T(4,128)(2,1)} async-done(((bf16[64,4,256]{2,1,0:T(4,128)(2,1)}), bf16[64,4,256]{2,1,0:T(4,128)(2,1)}, u32[]{:S(2)}, u32[]{:S(2)}) %all-to-all-start.6) | async-done | bytes 131104 | tf_op jit(solution)/shard_map/all_to_all | solution.py:24
  162.8 5.1 %all-to-all-start.7 = ((bf16[8,64,1280]{2,1,0:T(8,128)(2,1)}), bf16[8,64,1280]{2,1,0:T(8,128)(2,1)S(1)}, u32[]{:S(2)}, u32[]{:S(2)}) async-start(bf16[8,64,1280]{2,1,0:T(8,128)(2,1)} %fusion), calls=%async_computation.7 | async-start | bytes 2621440 | tf_op jit(solution)/shard_map/all_to_all | solution.py:24
  167.9 26.0 %all-gather = bf16[2048,64]{0,1:T(8,128)(2,1)} all-gather(bf16[512,64]{0,1:T(8,128)(2,1)S(1)} %get-tuple-element.23), channel_id=2, replica_groups=mesh['zh'=4,'y'=8,'x'=4,'zl'=2,'c'=2] {'zh'}, dimensions={0}, use_global_device_ids=true | all-gather | bytes 327680 | tf_op jit(solution)/shard_map/all_gather | solution.py:86
  193.9 1.8 reshape.260
  195.8 1.7 copy.87
  197.5 0.9 reshape.242
  198.4 1.9 convolution_convert_fusion.3
  200.3 0.9 reduce_sum.91
  201.2 0.8 slice_bitcast_fusion
  202.0 1.7 pad_maximum_fusion.1
  203.6 3.4 %all-to-all-start.8 = ((bf16[8,72,256]{2,1,0:T(8,128)(2,1)}), bf16[8,72,256]{2,1,0:T(8,128)(2,1)S(1)}, u32[]{:S(2)}, u32[]{:S(2)}) async-start(bf16[8,72,256]{2,1,0:T(8,128)(2,1)} %pad_maximum_fusion.1), calls=%async_computation.8 | async-start | bytes 589824 | tf_op jit(solution)/shard_map/all_to_all | solution.py:24
  207.1 0.9 slice.40
  208.2 0.3 copy.100
  208.5 0.4 reshape.247
  208.8 9.0 %all-to-all-done.8 = bf16[8,72,256]{2,1,0:T(8,128)(2,1)S(1)} async-done(((bf16[8,72,256]{2,1,0:T(8,128)(2,1)}), bf16[8,72,256]{2,1,0:T(8,128)(2,1)S(1)}, u32[]{:S(2)}, u32[]{:S(2)}) %all-to-all-start.8) | async-done | bytes 294944 | tf_op jit(solution)/shard_map/all_to_all | solution.py:24
  218.0 38.6 %all_to_all.50 = bf16[32,80,256]{2,1,0:T(8,128)(2,1)S(1)} all-to-all(bf16[32,80,256]{2,1,0:T(8,128)(2,1)S(1)} %pad_maximum_fusion), channel_id=1, replica_groups=mesh['zh'=4,'y'=8,'x'=4,'zl'=2,'c'=2] {'zh','y'}, dimensions={0} | all-to-all | bytes 2621440 | tf_op jit(solution)/shard_map/all_to_all | solution.py:24
  256.7 0.7 convert_reduce_fusion.2
  257.3 1.6 convert_bitcast_fusion
  259.0 0.7 copy.102
  259.7 2.9 %copy.101 = f32[8,64,4,256]{3,2,1,0:T(4,128)S(1)} copy(f32[8,64,4,256]{3,1,0,2:T(8,128)} %convert_bitcast_fusion) | data formatting | bytes 4194304 | tf_op jit(solution)/shard_map/reshape | solution.py:152
  262.6 1.8 copy.105
  (72 shorter events, 3.6 us)
Async XLA Ops:
  0.6 128.1 %copy-start = (bf16[1024,1024]{1,0:T(8,128)(2,1)S(1)}, bf16[1024,1024]{1,0:T(8,128)(2,1)}, u32[]{:S(2)}) copy-start(bf16[1024,1024]{1,0:T(8,128)(2,1)} %param.21) | copy-start | bytes 6291460
  2.5 24.6 %all-to-all-start.1 = ((bf16[8,64,512]{2,1,0:T(8,128)(2,1)}), bf16[8,64,512]{2,1,0:T(8,128)(2,1)S(1)}, u32[]{:S(2)}, u32[]{:S(2)}) async-start(bf16[8,64,512]{2,1,0:T(8,128)(2,1)} %broadcast_in_dim.44), calls=%async_computation.1 | async-start | bytes 1048576 | tf_op jit(solution)/shard_map/all_to_all | solution.py:24
  27.1 1.2 copy-start.4
  28.2 30.5 %all-to-all-start = ((bf16[4,512,256]{1,2,0:T(8,128)(2,1)}), bf16[4,512,256]{1,2,0:T(8,128)(2,1)S(1)}, u32[]{:S(2)}, u32[]{:S(2)}) async-start(bf16[4,512,256]{1,2,0:T(8,128)(2,1)} %broadcast_in_dim.43), calls=%async_computation | async-start | bytes 2097152 | tf_op jit(solution)/shard_map/all_to_all | solution.py:24
  60.5 1.0 copy-start.3
  61.5 3.8 %collective-permute-start = (bf16[8,64,512]{2,1,0:T(8,128)(2,1)S(1)}, bf16[8,64,512]{2,1,0:T(8,128)(2,1)S(1)}, u32[]{:S(2)}, u32[]{:S(2)}) collective-permute-start(bf16[8,64,512]{2,1,0:T(8,128)(2,1)S(1)} %dynamic-slice_bitcast_fusion.1), channel_id=1, source_target_pairs={{0,1},{1,0},{2,3},{3,2},{4,5},{5,4},{6,7},{7,6},{8,9},{9,8},{10,11... | collective-permute-start | bytes 1572872 | tf_op jit(solution)/shard_map/ppermute | solution.py:73
  67.3 27.2 %copy-start.8 = (bf16[64,4,8]{0,2,1:T(8,128)(2,1)S(1)}, bf16[64,4,8]{0,2,1:T(8,128)(2,1)}, u32[]{:S(2)}) copy-start(bf16[64,4,8]{0,2,1:T(8,128)(2,1)} %param.16) | copy-start | bytes 12292
  67.3 28.1 %copy-start.7 = (s32[64,25]{0,1:T(8,128)S(1)}, s32[64,25]{0,1:T(8,128)}, u32[]{:S(2)}) copy-start(s32[64,25]{0,1:T(8,128)} %param.17) | copy-start | bytes 19204
  67.3 21.6 %all-to-all-start.2 = ((bf16[8,64,512]{2,1,0:T(8,128)(2,1)}), bf16[8,64,512]{2,1,0:T(8,128)(2,1)S(1)}, u32[]{:S(2)}, u32[]{:S(2)}) async-start(bf16[8,64,512]{2,1,0:T(8,128)(2,1)} %fusion.11), calls=%async_computation.2 | async-start | bytes 1048576 | tf_op jit(solution)/shard_map/all_to_all | solution.py:24
  90.6 23.3 %copy-start.10 = (f32[512]{0:T(512)S(1)}, f32[512]{0:T(512)}, u32[]{:S(2)}) copy-start(f32[512]{0:T(512)} %param.15) | copy-start | bytes 6148
  90.6 16.4 %all-to-all-start.3 = ((bf16[32,2,2048]{2,1,0:T(2,128)(2,1)}), bf16[32,2,2048]{2,1,0:T(2,128)(2,1)S(1)}, u32[]{:S(2)}, u32[]{:S(2)}) async-start(bf16[32,2,2048]{2,1,0:T(2,128)(2,1)} %reshape.264), calls=%async_computation.3 | async-start | bytes 524288 | tf_op jit(solution)/shard_map/all_to_all | solution.py:24
  106.9 10.8 %all-to-all-start.5 = ((bf16[16,4,32]{2,1,0:T(4,128)(2,1)}), bf16[16,4,32]{2,1,0:T(4,128)(2,1)S(1)}, u32[]{:S(2)}, u32[]{:S(2)}) async-start(bf16[16,4,32]{2,1,0:T(4,128)(2,1)} %reshape.238), calls=%async_computation.5 | async-start | bytes 32768 | tf_op jit(solution)/shard_map/all_to_all | solution.py:24
  115.0 13.5 %copy-start.6 = (bf16[8,1024]{1,0:T(8,128)(2,1)S(1)}, bf16[8,1024]{1,0:T(8,128)(2,1)}, u32[]{:S(2)}) copy-start(bf16[8,1024]{1,0:T(8,128)(2,1)} %param.19) | copy-start | bytes 49156
  115.0 13.5 %copy-start.9 = (f32[1024]{0:T(1024)S(1)}, f32[1024]{0:T(1024)}, u32[]{:S(2)}) copy-start(f32[1024]{0:T(1024)} %param.20) | copy-start | bytes 12292
  117.7 10.2 %all-to-all-start.4 = ((bf16[16,4,1152]{2,1,0:T(4,128)(2,1)}), bf16[16,4,1152]{2,1,0:T(4,128)(2,1)S(1)}, u32[]{:S(2)}, u32[]{:S(2)}) async-start(bf16[16,4,1152]{2,1,0:T(4,128)(2,1)} %concatenate.16), calls=%async_computation.4 | async-start | bytes 294912 | tf_op jit(solution)/shard_map/all_to_all | solution.py:24
  123.7 5.0 %copy-start.11 = (f32[1024]{0:T(1024)S(1)}, f32[1024]{0:T(1024)}, u32[]{:S(2)}) copy-start(f32[1024]{0:T(1024)} %param.22) | copy-start | bytes 12292
  128.7 2.9 %copy-start.1 = (f32[256,1024]{1,0:T(8,128)}, f32[256,1024]{1,0:T(8,128)S(1)}, u32[]{:S(2)}) copy-start(f32[256,1024]{1,0:T(8,128)S(1)} %fusion.1) | copy-start | bytes 3145732
  128.8 1.3 copy-start.5
  131.7 0.8 copy-start.12
  139.7 4.6 %copy-start.2 = (f32[256,1024]{1,0:T(8,128)S(1)}, f32[256,1024]{1,0:T(8,128)}, u32[]{:S(2)}) copy-start(f32[256,1024]{1,0:T(8,128)} %copy-done.1) | copy-start | bytes 3145732
  139.7 4.6 %copy-start.13 = (bf16[256,1024]{1,0:T(8,128)(2,1)S(1)}, bf16[256,1024]{1,0:T(8,128)(2,1)}, u32[]{:S(2)}) copy-start(bf16[256,1024]{1,0:T(8,128)(2,1)} %copy-done.12) | copy-start | bytes 1572868
  142.3 11.2 %collective-permute-start.1 = (bf16[8,64,1280]{2,1,0:T(8,128)(2,1)}, bf16[8,64,1280]{2,1,0:T(8,128)(2,1)S(1)}, u32[]{:S(2)}, u32[]{:S(2)}) collective-permute-start(bf16[8,64,1280]{2,1,0:T(8,128)(2,1)} %dynamic-slice_bitcast_fusion), channel_id=1, source_target_pairs={{0,1},{1,0},{2,3},{3,2},{4,5},{5,4},{6,7},{7,6},{8,9},{9,8},{10,11... | collective-permute-start | bytes 3932168 | tf_op jit(solution)/shard_map/ppermute | solution.py:134
  146.1 16.7 %all-to-all-start.6 = ((bf16[64,4,256]{2,1,0:T(4,128)(2,1)}), bf16[64,4,256]{2,1,0:T(4,128)(2,1)}, u32[]{:S(2)}, u32[]{:S(2)}) async-start(bf16[64,4,256]{2,1,0:T(4,128)(2,1)} %bitcast.103), calls=%async_computation.6 | async-start | bytes 262144 | tf_op jit(solution)/shard_map/all_to_all | solution.py:24
  162.8 37.5 %all-to-all-start.7 = ((bf16[8,64,1280]{2,1,0:T(8,128)(2,1)}), bf16[8,64,1280]{2,1,0:T(8,128)(2,1)S(1)}, u32[]{:S(2)}, u32[]{:S(2)}) async-start(bf16[8,64,1280]{2,1,0:T(8,128)(2,1)} %fusion), calls=%async_computation.7 | async-start | bytes 2621440 | tf_op jit(solution)/shard_map/all_to_all | solution.py:24
  203.6 14.2 %all-to-all-start.8 = ((bf16[8,72,256]{2,1,0:T(8,128)(2,1)}), bf16[8,72,256]{2,1,0:T(8,128)(2,1)S(1)}, u32[]{:S(2)}, u32[]{:S(2)}) async-start(bf16[8,72,256]{2,1,0:T(8,128)(2,1)} %pad_maximum_fusion.1), calls=%async_computation.8 | async-start | bytes 589824 | tf_op jit(solution)/shard_map/all_to_all | solution.py:24

commit v2 on v1

v2 whole, which is shorter than its diff:
```python
import jax
import jax.numpy as jnp
from jax import lax
from jax.experimental import pallas as pl
from jax.experimental.pallas import tpu as pltpu
from jax.sharding import Mesh, PartitionSpec as P

NORM_EPS = 1e-05
bf16, f32 = jnp.bfloat16, jnp.float32
DP = ("zh", "y")
TENSOR = ("x", "zl", "c")
PARTS = {"zh": 4, "y": 8, "x": 4, "zl": 2, "c": 2}


def swish_slope(values, sig):
    return sig * (1.0 + values * (1.0 - sig))


def contract(left, right, left_dim, right_dim):
    return lax.dot_general(
        left, right, (((left_dim,), (right_dim,)), ((), ())), preferred_element_type=f32
    )


def exchange(blocks, axes):
    return lax.all_to_all(blocks, axes, 0, 0, tiled=True)


def spread(block, axes, count):
    return exchange(jnp.broadcast_to(block[None], (count,) + block.shape), axes)


def from_others(block, axis, count):
    return [
        lax.ppermute(block, axis, [(i, (i - k) % count) for i in range(count)])
        for k in range(1, count)
    ]


def finish_body(blocks_ref, first_ref, output_ref, hidden_ref):
    n_zh, n_y = PARTS["zh"], PARTS["y"]
    for y in range(n_y):
        for zh in range(n_zh):
            first_ref[64 * y : 64 * (y + 1), 256 * zh : 256 * (zh + 1)] = blocks_ref[
                n_y * zh + y, :64, :
            ].astype(f32)
    extra = blocks_ref[:, 64:80, :].astype(f32)
    for y in range(n_y):
        total = extra[y]
        for zh in range(1, n_zh):
            total = total + extra[n_y * zh + y]
        output_ref[8 * y : 8 * (y + 1), :] = total[:8, :200]
    hidden_ref[...] = jnp.sum(extra, axis=0)[8:]


def epinet_body(
    first_ref,
    index_ref,
    bias_first_ref,
    w_hidden_ref,
    bias_hidden_ref,
    w_output_ref,
    targets_ref,
    same_ref,
    row_ref,
    act_first_ref,
    second_grad_ref,
    act_second_ref,
    out_cot_ref,
    draws_ref,
):
    n_t, own, _ = first_ref.shape
    hidden = w_hidden_ref.shape[0]
    idx = index_ref.shape[0]
    pairs = act_first_ref.shape[0]
    lanes = pairs // (n_t * own)
    total = first_ref[0]
    for t in range(n_t):
        draws_ref[own * t : own * (t + 1), :] = first_ref[t, :, hidden:]
        if t:
            total = total + first_ref[t]
    draws = draws_ref[...]
    draws = jnp.concatenate([draws[:, idx * s : idx * (s + 1)] for s in range(lanes)], axis=0)
    spread_draws = jnp.dot(draws.astype(bf16), index_ref[...], preferred_element_type=f32)
    index_term, draws_rep = spread_draws[:, :hidden], spread_draws[:, hidden:]
    square_sum = total[:, hidden + idx * lanes : hidden + idx * lanes + 1]
    scale = lax.rsqrt(square_sum / (n_t * 512) + NORM_EPS)
    first_pre = total[:, :hidden] * scale + bias_first_ref[...]

    def per_pair(values):
        twice = jnp.concatenate([values, values], axis=0)
        twice = jnp.broadcast_to(twice[None], (pairs // (2 * own),) + twice.shape)
        return twice.reshape(pairs, values.shape[1])

    pre_first = per_pair(first_pre) + index_term
    sig_first = jax.nn.sigmoid(pre_first)
    act_first = (pre_first * sig_first).astype(bf16)
    act_first_ref[...] = act_first
    pre_second = (
        jnp.dot(act_first, w_hidden_ref[...], preferred_element_type=f32) + bias_hidden_ref[...]
    )
    sig_second = jax.nn.sigmoid(pre_second)
    act_second = (pre_second * sig_second).astype(bf16)
    act_second_ref[...] = act_second
    readout = jnp.dot(act_second, w_output_ref[...], preferred_element_type=f32)
    logits = jnp.dot(
        readout * draws_rep,
        same_ref[...],
        precision=lax.Precision.HIGHEST,
        preferred_element_type=f32,
    )
    logit_grad = (jax.nn.sigmoid(logits) - per_pair(targets_ref[...])) / (n_t * lanes)
    out_cot = (logit_grad * draws_rep).astype(bf16)
    out_cot_ref[...] = out_cot
    second_grad = (
        contract(out_cot, w_output_ref[...], 1, 1) * swish_slope(pre_second, sig_second)
    ).astype(bf16)
    second_grad_ref[...] = second_grad
    first_grad = contract(second_grad, w_hidden_ref[...], 1, 1) * swish_slope(pre_first, sig_first)
    first_grad = first_grad.astype(bf16).astype(f32)
    row_sum = jnp.sum(first_grad.reshape(pairs // (2 * own), 2 * own, hidden), axis=0)
    row_grad = (row_sum[:own] + row_sum[own:]) * scale
    row_grad = row_grad.astype(bf16)
    for t in range(n_t):
        row_ref[t] = row_grad


def weights_body(core_ref, act_first_ref, second_grad_ref, act_second_ref, out_cot_ref, mine_ref, other_ref):
    hidden = second_grad_ref.shape[1]
    blocks, rows, _ = mine_ref.shape
    low_core = core_ref[0] == 0
    for i in range(blocks):
        at = slice(2 * rows * i, 2 * rows * (i + 1))
        for left_ref, right_ref, to in (
            (act_first_ref, second_grad_ref, slice(0, hidden)),
            (act_second_ref, out_cot_ref, slice(hidden, hidden + 256)),
        ):
            both = contract(left_ref[:, at], right_ref[...], 0, 0)
            mine_ref[i, :, to] = jnp.where(low_core, both[:rows], both[rows:]).astype(bf16)
            other_ref[i, :, to] = jnp.where(low_core, both[rows:], both[:rows]).astype(bf16)


def shards(
    residual,
    attention,
    out_proj,
    norm_gain,
    index_draws,
    labels,
    w_first,
    w_index,
    bias_first,
    w_hidden,
    bias_hidden,
    w_output,
):
    rows, width = residual.shape
    n_zh, n_y, n_t = PARTS["zh"], PARTS["y"], 16
    zh = lax.axis_index("zh")
    y, zl, c = lax.axis_index("y"), lax.axis_index("zl"), lax.axis_index("c")
    tensor = lax.axis_index(TENSOR)
    cols = out_proj.shape[1]
    quarter = cols // 4
    own = rows // n_t
    samples = index_draws.shape[1] * n_t
    idx = index_draws.shape[2]
    hidden = w_hidden.shape[0]
    classes = labels.shape[1]
    reads = classes * idx

    lanes = jnp.arange(256)
    real = lanes < reads
    tile = ((lanes[None, :] % idx == jnp.arange(idx)[:, None]) & real[None, :]).astype(bf16)
    index_weights = jnp.concatenate([w_index, tile], axis=1)
    same = (lanes[:, None] // idx == lanes[None, :] // idx).astype(f32)
    w_output_wide = jnp.pad(w_output, ((0, 0), (0, 256 - reads)))
    own_labels = lax.dynamic_slice_in_dim(labels, tensor * own, own, 0).astype(f32)
    targets = jnp.broadcast_to(own_labels[:, :, None], (own, classes, idx)).reshape(own, reads)
    targets = jnp.pad(targets, ((0, 0), (0, 256 - reads)))
    att = spread(attention, "y", n_y).reshape(n_y * rows, width)
    part = jnp.zeros((n_zh, cols, n_y * rows), bf16)
    for k, proj in enumerate([out_proj] + from_others(out_proj, "zh", n_zh)):
        one = contract(proj, att, 0, 1).astype(bf16)
        part = lax.dynamic_update_index_in_dim(part, one, (zh + k) % n_zh, 0)
    part = part.reshape(n_zh * 2, 2, quarter, n_y * rows)
    mine = lax.dynamic_index_in_dim(part, c, 1, keepdims=False)
    other = lax.dynamic_index_in_dim(part, 1 - c, 1, keepdims=False)
    swapped = lax.ppermute(other, "c", [(0, 1), (1, 0)])
    pair = (mine.astype(f32) + swapped.astype(f32)).astype(bf16)
    branch = jnp.sum(exchange(pair, ("x", "zl")).astype(f32), axis=0).astype(bf16)
    branch = branch.reshape(quarter, n_y, rows).transpose(1, 0, 2)
    slot = (jnp.arange(4) == y // 2)[None, :, None, None]
    branch = jnp.where(slot, branch[:, None], jnp.zeros((), bf16))
    branch = exchange(branch.reshape(n_y * 4, quarter, rows), ("y", "zl", "c"))
    branch = branch.reshape(n_y, 4 * quarter, rows)
    branch = lax.dynamic_slice_in_dim(branch, 2 * (2 * zl + c), 2, 0).reshape(width, rows)

    state = residual.astype(f32).T + branch.astype(f32)
    square_sum = jnp.sum(state * state, axis=0)
    gained = (state * norm_gain[:, None]).astype(bf16).T
    first = jnp.dot(gained, w_first, preferred_element_type=f32)
    own_draws = samples // n_t * idx
    extra = jnp.concatenate(
        [
            index_draws.reshape(rows, own_draws).astype(f32),
            square_sum[:, None],
            jnp.zeros((rows, 127 - own_draws), f32),
        ],
        axis=1,
    )
    first = jnp.concatenate([first, extra], axis=1).reshape(n_t, own, hidden + 128)
    first = exchange(first, TENSOR)

    pairs = own * samples
    by_pair = jax.ShapeDtypeStruct((pairs, hidden), bf16)
    row_grad, act_first, second_grad, act_second, out_cot = pl.pallas_call(
        epinet_body,
        out_shape=(
            jax.ShapeDtypeStruct((n_t, own, hidden), bf16),
            by_pair,
            by_pair,
            by_pair,
            jax.ShapeDtypeStruct((pairs, 256), bf16),
        ),
        scratch_shapes=[pltpu.VMEM((rows, 128), f32)],
        compiler_params=pltpu.CompilerParams(vmem_limit_bytes=32 * 2**20),
        cost_estimate=pl.CostEstimate(
            flops=2 * 10**9, bytes_accessed=8 * 2**20, transcendentals=2**20
        ),
    )(
        first,
        index_weights,
        bias_first[None],
        w_hidden,
        bias_hidden[None],
        w_output_wide,
        targets,
        same,
    )

    row_blocks = exchange(row_grad, TENSOR).reshape(rows, n_zh, cols).transpose(1, 0, 2)
    both = jnp.broadcast_to(gained[None], (n_zh, rows, width))
    both = exchange(jnp.concatenate([both, row_blocks], axis=2), "zh").reshape(n_zh * rows, -1)
    gained_all, row_blocks = both[:, :width], both[:, width:]

    half = jax.ShapeDtypeStruct((n_t // 2, hidden // n_t, hidden + 256), bf16)
    vmem = pl.BlockSpec(memory_space=pltpu.VMEM)
    mine, other = pl.pallas_call(
        weights_body,
        out_shape=(half, half),
        in_specs=[pl.BlockSpec(memory_space=pltpu.SMEM)] + [vmem] * 4,
        compiler_params=pltpu.CompilerParams(vmem_limit_bytes=32 * 2**20),
        cost_estimate=pl.CostEstimate(
            flops=7 * 10**8, bytes_accessed=4 * 2**20, transcendentals=0
        ),
    )(c.reshape(1), act_first, second_grad, act_second, out_cot)
    swapped = lax.ppermute(other, "c", [(0, 1), (1, 0)])
    weights = (mine.astype(f32) + swapped.astype(f32)).astype(bf16)
    weights = jnp.sum(exchange(weights, ("x", "zl")).astype(f32), axis=0).astype(bf16)
    hidden_rows = hidden // n_t
    output_rows = weights[:, hidden:].reshape(n_y, hidden_rows // n_y, 256)
    hidden_cols = hidden // (n_zh * n_y)
    hidden_blocks = weights[:, :hidden].T.reshape(n_zh * n_y, 4, 8, hidden_rows)
    hidden_blocks = hidden_blocks.transpose(0, 2, 1, 3).reshape(n_zh * n_y, 8, 256)

    grads = contract(gained_all, row_blocks, 0, 0).astype(bf16)
    grads = jnp.concatenate([grads.reshape(n_y, width // n_y, cols), output_rows], axis=1)
    grads = jnp.sum(exchange(grads, "y").astype(f32), axis=0).astype(bf16)

    grads = jnp.broadcast_to(grads[None], (n_zh * n_y,) + grads.shape)
    grads = exchange(jnp.concatenate([grads, hidden_blocks], axis=1), DP)
    grad_first, grad_output, grad_hidden = pl.pallas_call(
        finish_body,
        out_shape=(
            jax.ShapeDtypeStruct((width, hidden), f32),
            jax.ShapeDtypeStruct((hidden_rows, reads), f32),
            jax.ShapeDtypeStruct((8, 256), f32),
        ),
        compiler_params=pltpu.CompilerParams(vmem_limit_bytes=24 * 2**20),
        cost_estimate=pl.CostEstimate(flops=0, bytes_accessed=4 * 2**20, transcendentals=0),
    )(grads)
    grad_hidden = grad_hidden.reshape(8, 4, hidden_rows).transpose(2, 1, 0)
    return (grad_first, grad_hidden.reshape(hidden_rows, hidden_cols), grad_output)


def solution(mesh):
    fine = Mesh(mesh.devices.reshape(tuple(PARTS.values())), tuple(PARTS))
    placed = (
        P(DP, TENSOR),
        P(DP, TENSOR),
        P(TENSOR, DP),
        P(TENSOR),
        P(DP, TENSOR, None),
        P(DP, None),
        P(TENSOR, None),
        P(),
        P(),
        P(),
        P(),
        P(),
    )
    return jax.shard_map(
        shards,
        mesh=fine,
        in_specs=placed,
        out_specs=(P(TENSOR, None), P(TENSOR, DP), P(TENSOR, None)),
        check_vma=False,
    )
```

time: 267 us -> 223 us (0.84)
  local copies, waits for them, and re-layouts: 32.1 us -> 9.52 us
  blocking collectives: 64.6 us -> 53 us
  other arithmetic: 13.2 us -> 5.96 us
  matrix products: 10.1 us -> 2.92 us
  Pallas kernels: 0 us -> 6.17 us
    all_gather x1 -> x0, blocking collectives: 26 us -> none  [shards(): gained_all = lax.all_gather(gained, 'zh', axis=0)]
    all_to_all x9 -> x7, starting transfers between devices: 62.4 us -> 43.6 us  [exchange(): return lax.all_to_all(blocks, axes, 0, 0, tiled=True)]
    ppermute x0 -> x3, starting transfers between devices: none -> 17.7 us  [from_others(): lax.ppermute(block, axis, [(i, (i - k) % count) for i in range(count)])]
    ppermute x0 -> x3, waiting for transfers between devices: none -> 14.9 us  [from_others(): lax.ppermute(block, axis, [(i, (i - k) % count) for i in range(count)])]
    all_to_all x9 -> x7, waiting for transfers between devices: 75.1 us -> 60.2 us  [exchange(): return lax.all_to_all(blocks, axes, 0, 0, tiled=True)]
    all_to_all x1 -> x2, blocking collectives: 38.6 us -> 53 us  [exchange(): return lax.all_to_all(blocks, axes, 0, 0, tiled=True)]
    pallas_call x0 -> x3, Pallas kernels: none -> 6.17 us  [the longest x1 2.71 us: shards(): pl.pallas_call(epinet_body, out_shape=(jax.ShapeDtypeStruct((n_t, own, hi...]
    reshape x5 -> x4, local copies, waits for them, and re-layouts: 5.02 us -> 0.45 us  [the longest x1 0.21 us: shards(): hidden_blocks.transpose(0, 2, 1, 3).reshape(n_zh * n_y, 8, 256)]
  transfers between devices with their start and end apart: 11 -> 12, of which waited for: 8 -> 8; matrix products, arithmetic and copies ran while one was open for 8% -> 3% of each run, Pallas kernels for 0% -> 0%
where the time goes in v2:
time: 223 us; the launch traced here: 221 us
  waiting for transfers between devices  77 us (35%)
  starting transfers between devices  65.1 us (29%)
  blocking collectives  53 us (24%)
  local copies, waits for them, and re-layouts  9.52 us (4%)
  Pallas kernels  6.17 us (3%)
  other arithmetic  5.96 us (3%)
  matrix products  2.92 us (1%)
    all_to_all x7, waiting for transfers between devices, exchange(): return lax.all_to_all(blocks, axes, 0, 0, tiled=True)  60.2 us
    all_to_all x2, blocking collectives, exchange(): return lax.all_to_all(blocks, axes, 0, 0, tiled=True)  53 us
    all_to_all x7, starting transfers between devices, exchange(): return lax.all_to_all(blocks, axes, 0, 0, tiled=True)  43.6 us
    ppermute x3, starting transfers between devices, from_others(): lax.ppermute(block, axis, [(i, (i - k) % count) for i in range(count)])  17.7 us
    ppermute x3, waiting for transfers between devices, from_others(): lax.ppermute(block, axis, [(i, (i - k) % count) for i in range(count)])  14.9 us
  transfers between devices with their start and end apart: 12, of which 8 were waited for; matrix products, arithmetic and copies ran while one was open for 3% of the time, Pallas kernels for 0%

profile of v2, /device:TPU:6, one launch (start us, length us, event | category | flops | bytes accessed | tf_op | source)
XLA Modules:
  0.0 220.8 jit_solution(10660320737828602805)
XLA Ops:
  0.7 1.8 broadcast_in_dim.88
  2.4 7.1 %all-to-all-start = ((bf16[8,64,512]{2,1,0:T(8,128)(2,1)}), bf16[8,64,512]{2,1,0:T(8,128)(2,1)S(1)}, u32[]{:S(2)}, u32[]{:S(2)}) async-start(bf16[8,64,512]{2,1,0:T(8,128)(2,1)} %broadcast_in_dim.88), calls=%async_computation | async-start | bytes 1048576 | tf_op jit(solution)/shard_map/all_to_all | solution.py:26
  9.5 10.9 %collective-permute-start = (bf16[512,256]{1,0:T(8,128)(2,1)S(1)}, bf16[512,256]{1,0:T(8,128)(2,1)}, u32[]{:S(2)}, u32[]{:S(2)}) collective-permute-start(bf16[512,256]{1,0:T(8,128)(2,1)S(1)} %copy-done.5), channel_id=1, source_target_pairs={{0,384},{128,0},{256,128},{384,256},{1,385},{129,1},{257,129},{385... | collective-permute-start | bytes 786440 | tf_op jit(solution)/shard_map/ppermute | solution.py:35
  20.5 1.9 collective-permute-start.1
  22.4 4.8 %collective-permute-start.2 = (bf16[512,256]{1,0:T(8,128)(2,1)S(1)}, bf16[512,256]{1,0:T(8,128)(2,1)S(1)}, u32[]{:S(2)}, u32[]{:S(2)}) collective-permute-start(bf16[512,256]{1,0:T(8,128)(2,1)S(1)} %copy-done.5), channel_id=1, source_target_pairs={{0,128},{128,256},{256,384},{384,0},{1,129},{129,257},{257,385},{3... | collective-permute-start | bytes 786440 | tf_op jit(solution)/shard_map/ppermute | solution.py:35
  27.3 0.1 broadcast_in_dim.87
  27.4 0.3 fusion.1
  27.7 14.9 %collective-permute-done = bf16[512,256]{1,0:T(8,128)(2,1)} collective-permute-done((bf16[512,256]{1,0:T(8,128)(2,1)S(1)}, bf16[512,256]{1,0:T(8,128)(2,1)}, u32[]{:S(2)}, u32[]{:S(2)}) %collective-permute-start) | collective-permute-done | bytes 262176 | tf_op jit(solution)/shard_map/ppermute | solution.py:35
  42.6 1.3 fusion.3
  43.9 0.4 fusion.5
  44.3 0.4 fusion.7
  44.7 1.9 collective-permute-start.3
  46.6 1.9 collective-permute-done.3
  48.5 0.9 fusion.8
  49.4 7.0 %all-to-all-start.1 = ((bf16[8,64,512]{2,1,0:T(8,128)(2,1)}), bf16[8,64,512]{2,1,0:T(8,128)(2,1)S(1)}, u32[]{:S(2)}, u32[]{:S(2)}) async-start(bf16[8,64,512]{2,1,0:T(8,128)(2,1)} %fusion.8), calls=%async_computation.1 | async-start | bytes 1048576 | tf_op jit(solution)/shard_map/all_to_all | solution.py:26
  56.4 0.1 broadcast_in_dim.85
  56.5 0.1 copy.60
  56.6 0.1 reshape.185
  56.8 0.2 copy.62
  57.0 0.1 pad.8.w_output_ref
  57.1 7.3 %all-to-all-done.1 = bf16[8,64,512]{2,1,0:T(8,128)(2,1)S(1)} async-done(((bf16[8,64,512]{2,1,0:T(8,128)(2,1)}), bf16[8,64,512]{2,1,0:T(8,128)(2,1)S(1)}, u32[]{:S(2)}, u32[]{:S(2)}) %all-to-all-start.1) | async-done | bytes 524320 | tf_op jit(solution)/shard_map/all_to_all | solution.py:26
  64.5 0.1 reshape.171
  64.6 0.2 copy.58
  64.8 0.1 bitcast_select_fusion
  64.9 1.1 reshape.186
  66.0 7.9 %all-to-all-start.2 = ((bf16[32,2,2048]{2,1,0:T(2,128)(2,1)}), bf16[32,2,2048]{2,1,0:T(2,128)(2,1)S(1)}, u32[]{:S(2)}, u32[]{:S(2)}) async-start(bf16[32,2,2048]{2,1,0:T(2,128)(2,1)} %reshape.186), calls=%async_computation.2 | async-start | bytes 524288 | tf_op jit(solution)/shard_map/all_to_all | solution.py:26
  73.9 0.1 constant_dynamic-slice_fusion
  74.0 0.1 copy.68
  74.2 0.1 reshape.173
  74.3 11.8 %all-to-all-done.2 = bf16[32,2,2048]{2,1,0:T(2,128)(2,1)S(1)} async-done(((bf16[32,2,2048]{2,1,0:T(2,128)(2,1)}), bf16[32,2,2048]{2,1,0:T(2,128)(2,1)S(1)}, u32[]{:S(2)}, u32[]{:S(2)}) %all-to-all-start.2) | async-done | bytes 262176 | tf_op jit(solution)/shard_map/all_to_all | solution.py:26
  86.1 0.4 reshape.187
  86.5 0.3 copy.59
  86.9 0.3 reshape.172
  87.3 0.1 multiply_reduce_fusion
  87.5 0.3 fusion.14
  87.9 0.2 concatenate.27
  88.1 0.9 concatenate.22
  89.0 5.6 %all-to-all-start.3 = ((f32[16,4,1152]{2,1,0:T(4,128)}), f32[16,4,1152]{2,1,0:T(4,128)S(1)}, u32[]{:S(2)}, u32[]{:S(2)}) async-start(f32[16,4,1152]{2,1,0:T(4,128)} %concatenate.22), calls=%async_computation.3 | async-start | bytes 589824 | tf_op jit(solution)/shard_map/all_to_all | solution.py:26
  94.6 0.1 compare_convert_fusion.same_ref
  94.7 6.0 %all-to-all-done.3.first_ref = f32[16,4,1152]{2,1,0:T(4,128)S(1)} async-done(((f32[16,4,1152]{2,1,0:T(4,128)}), f32[16,4,1152]{2,1,0:T(4,128)S(1)}, u32[]{:S(2)}, u32[]{:S(2)}) %all-to-all-start.3) | async-done | bytes 294944 | tf_op jit(solution)/shard_map/all_to_all | solution.py:26
  100.7 1.6 copy-done.1
  102.3 2.7 %shard_map.139 = (bf16[16,4,1024]{2,1,0:T(4,128)(2,1)S(1)}, bf16[256,1024]{1,0:T(8,128)(2,1)S(1)}, bf16[256,1024]{1,0:T(8,128)(2,1)S(1)}, bf16[256,1024]{1,0:T(8,128)(2,1)S(1)}, bf16[256,256]{1,0:T(8,128)(2,1)S(1)}) custom-call(f32[16,4,1152]{2,1,0:T(4,128)S(1)} %all-to-all-done.3.first_ref, bf16[8,1280]{1,0:T(8,128)(2,1)S(1)} %pad_maximum_fusion.3.index_ref, ...), custom_call_target="tpu_custom_call" | custom-call | flops 2000000000 | bytes 8388608 | tf_op jit(solution)/shard_map/pallas_call | solution.py:216
  105.0 2.0 shard_map.140
  107.0 1.9 collective-permute-start.4
  108.9 9.2 %all_to_all.45 = bf16[16,4,1024]{2,1,0:T(4,128)(2,1)S(1)} all-to-all(bf16[16,4,1024]{2,1,0:T(4,128)(2,1)S(1)} %get-tuple-element.13), channel_id=1, replica_groups=mesh['zh'=4,'y'=8,'x'=4,'zl'=2,'c'=2] {'x','zl','c'}, dimensions={0} | all-to-all | bytes 262144 | tf_op jit(solution)/shard_map/all_to_all | solution.py:26
  118.3 0.8 pad_maximum_fusion.1
  119.1 6.9 %all-to-all-start.5 = ((bf16[4,64,768]{2,1,0:T(8,128)(2,1)}), bf16[4,64,768]{2,1,0:T(8,128)(2,1)S(1)}, u32[]{:S(2)}, u32[]{:S(2)}) async-start(bf16[4,64,768]{2,1,0:T(8,128)(2,1)} %pad_maximum_fusion.1), calls=%async_computation.5 | async-start | bytes 786432 | tf_op jit(solution)/shard_map/all_to_all | solution.py:26
  125.9 2.7 %add_convert_fusion = bf16[8,64,1280]{2,1,0:T(8,128)(2,1)} fusion(bf16[8,64,1280]{2,1,0:T(8,128)(2,1)} %collective-permute-done.4, bf16[8,64,1280]{2,1,0:T(8,128)(2,1)S(1)} %get-tuple-element.18), kind=kLoop, calls=%fused_computation | loop fusion | flops 2621440 | bytes 3932160 | tf_op jit(solution)/shard_map/convert_element_type | solution.py:258
  128.6 10.5 %all-to-all-done.5 = bf16[4,64,768]{2,1,0:T(8,128)(2,1)S(1)} async-done(((bf16[4,64,768]{2,1,0:T(8,128)(2,1)}), bf16[4,64,768]{2,1,0:T(8,128)(2,1)S(1)}, u32[]{:S(2)}, u32[]{:S(2)}) %all-to-all-start.5) | async-done | bytes 393248 | tf_op jit(solution)/shard_map/all_to_all | solution.py:26
  139.1 5.7 %all-to-all-start.6 = ((bf16[8,64,1280]{2,1,0:T(8,128)(2,1)}), bf16[8,64,1280]{2,1,0:T(8,128)(2,1)S(1)}, u32[]{:S(2)}, u32[]{:S(2)}) async-start(bf16[8,64,1280]{2,1,0:T(8,128)(2,1)} %add_convert_fusion), calls=%async_computation.6 | async-start | bytes 2621440 | tf_op jit(solution)/shard_map/all_to_all | solution.py:26
  144.8 0.3 convolution_convert_fusion
  145.0 14.4 %all-to-all-done.6 = bf16[8,64,1280]{2,1,0:T(8,128)(2,1)S(1)} async-done(((bf16[8,64,1280]{2,1,0:T(8,128)(2,1)}), bf16[8,64,1280]{2,1,0:T(8,128)(2,1)S(1)}, u32[]{:S(2)}, u32[]{:S(2)}) %all-to-all-start.6) | async-done | bytes 1310752 | tf_op jit(solution)/shard_map/all_to_all | solution.py:26
  159.5 0.2 reduce_sum.47
  159.7 0.7 pad_maximum_fusion.2
  160.4 3.4 %all-to-all-start.7 = ((bf16[8,72,256]{2,1,0:T(8,128)(2,1)}), bf16[8,72,256]{2,1,0:T(8,128)(2,1)S(1)}, u32[]{:S(2)}, u32[]{:S(2)}) async-start(bf16[8,72,256]{2,1,0:T(8,128)(2,1)} %pad_maximum_fusion.2), calls=%async_computation.7 | async-start | bytes 589824 | tf_op jit(solution)/shard_map/all_to_all | solution.py:26
  163.9 0.2 copy.65
  164.0 0.1 copy.66
  164.2 0.2 reshape.180
  164.4 10.2 %all-to-all-done.7 = bf16[8,72,256]{2,1,0:T(8,128)(2,1)S(1)} async-done(((bf16[8,72,256]{2,1,0:T(8,128)(2,1)}), bf16[8,72,256]{2,1,0:T(8,128)(2,1)S(1)}, u32[]{:S(2)}, u32[]{:S(2)}) %all-to-all-start.7) | async-done | bytes 294944 | tf_op jit(solution)/shard_map/all_to_all | solution.py:26
  174.6 0.1 broadcast_in_dim.101
  174.7 0.1 pad_maximum_fusion
  174.8 43.8 %all_to_all.46.blocks_ref = bf16[32,80,256]{2,1,0:T(8,128)(2,1)S(1)} all-to-all(bf16[32,80,256]{2,1,0:T(8,128)(2,1)S(1)} %pad_maximum_fusion), channel_id=1, replica_groups=mesh['zh'=4,'y'=8,'x'=4,'zl'=2,'c'=2] {'zh','y'}, dimensions={0} | all-to-all | bytes 2621440 | tf_op jit(solution)/shard_map/all_to_all | solution.py:26
  218.6 1.5 shard_map.141
  220.2 0.6 copy.71
  (48 shorter events, 0.7 us)
Async XLA Ops:
  0.6 86.8 %copy-start = (bf16[512,1024]{1,0:T(8,128)(2,1)S(1)}, bf16[512,1024]{1,0:T(8,128)(2,1)}, u32[]{:S(2)}) copy-start(bf16[512,1024]{1,0:T(8,128)(2,1)} %param.18) | copy-start | bytes 3145732
  0.6 8.9 %copy-start.5 = (bf16[512,256]{1,0:T(8,128)(2,1)S(1)}, bf16[512,256]{1,0:T(8,128)(2,1)}, u32[]{:S(2)}) copy-start(bf16[512,256]{1,0:T(8,128)(2,1)} %param.14) | copy-start | bytes 786436
  2.4 24.9 %all-to-all-start = ((bf16[8,64,512]{2,1,0:T(8,128)(2,1)}), bf16[8,64,512]{2,1,0:T(8,128)(2,1)S(1)}, u32[]{:S(2)}, u32[]{:S(2)}) async-start(bf16[8,64,512]{2,1,0:T(8,128)(2,1)} %broadcast_in_dim.88), calls=%async_computation | async-start | bytes 1048576 | tf_op jit(solution)/shard_map/all_to_all | solution.py:26
  9.5 33.1 %collective-permute-start = (bf16[512,256]{1,0:T(8,128)(2,1)S(1)}, bf16[512,256]{1,0:T(8,128)(2,1)}, u32[]{:S(2)}, u32[]{:S(2)}) collective-permute-start(bf16[512,256]{1,0:T(8,128)(2,1)S(1)} %copy-done.5), channel_id=1, source_target_pairs={{0,384},{128,0},{256,128},{384,256},{1,385},{129,1},{257,129},{385... | collective-permute-start | bytes 786440 | tf_op jit(solution)/shard_map/ppermute | solution.py:35
  20.5 23.4 %collective-permute-start.1 = (bf16[512,256]{1,0:T(8,128)(2,1)S(1)}, bf16[512,256]{1,0:T(8,128)(2,1)S(1)}, u32[]{:S(2)}, u32[]{:S(2)}) collective-permute-start(bf16[512,256]{1,0:T(8,128)(2,1)S(1)} %copy-done.5), channel_id=1, source_target_pairs={{0,256},{128,384},{256,0},{384,128},{1,257},{129,385},{257,1},{385... | collective-permute-start | bytes 786440 | tf_op jit(solution)/shard_map/ppermute | solution.py:35
  22.4 21.9 %collective-permute-start.2 = (bf16[512,256]{1,0:T(8,128)(2,1)S(1)}, bf16[512,256]{1,0:T(8,128)(2,1)S(1)}, u32[]{:S(2)}, u32[]{:S(2)}) collective-permute-start(bf16[512,256]{1,0:T(8,128)(2,1)S(1)} %copy-done.5), channel_id=1, source_target_pairs={{0,128},{128,256},{256,384},{384,0},{1,129},{129,257},{257,385},{3... | collective-permute-start | bytes 786440 | tf_op jit(solution)/shard_map/ppermute | solution.py:35
  44.7 3.8 %collective-permute-start.3 = (bf16[8,64,512]{2,1,0:T(8,128)(2,1)S(1)}, bf16[8,64,512]{2,1,0:T(8,128)(2,1)S(1)}, u32[]{:S(2)}, u32[]{:S(2)}) collective-permute-start(bf16[8,64,512]{2,1,0:T(8,128)(2,1)S(1)} %dynamic-slice_bitcast_fusion), channel_id=1, source_target_pairs={{0,1},{1,0},{2,3},{3,2},{4,5},{5,4},{6,7},{7,6},{8,9},{9,8},{10,11... | collective-permute-start | bytes 1572872 | tf_op jit(solution)/shard_map/ppermute | solution.py:188
  46.6 10.1 %copy-start.4 = (bf16[1024,200]{0,1:T(8,128)(2,1)S(1)}, bf16[1024,200]{0,1:T(8,128)(2,1)}, u32[]{:S(2)}) copy-start(bf16[1024,200]{0,1:T(8,128)(2,1)} %param.23) | copy-start | bytes 1228804
  48.5 8.0 %copy-start.9 = (bf16[64,4,8]{0,2,1:T(8,128)(2,1)S(1)}, bf16[64,4,8]{0,2,1:T(8,128)(2,1)}, u32[]{:S(2)}) copy-start(bf16[64,4,8]{0,2,1:T(8,128)(2,1)} %param.16) | copy-start | bytes 12292
  49.4 15.0 %all-to-all-start.1 = ((bf16[8,64,512]{2,1,0:T(8,128)(2,1)}), bf16[8,64,512]{2,1,0:T(8,128)(2,1)S(1)}, u32[]{:S(2)}, u32[]{:S(2)}) async-start(bf16[8,64,512]{2,1,0:T(8,128)(2,1)} %fusion.8), calls=%async_computation.1 | async-start | bytes 1048576 | tf_op jit(solution)/shard_map/all_to_all | solution.py:26
  64.5 9.4 %copy-start.7 = (s32[64,25]{0,1:T(8,128)S(1)}, s32[64,25]{0,1:T(8,128)}, u32[]{:S(2)}) copy-start(s32[64,25]{0,1:T(8,128)} %param.17) | copy-start | bytes 19204
  66.0 20.1 %all-to-all-start.2 = ((bf16[32,2,2048]{2,1,0:T(2,128)(2,1)}), bf16[32,2,2048]{2,1,0:T(2,128)(2,1)S(1)}, u32[]{:S(2)}, u32[]{:S(2)}) async-start(bf16[32,2,2048]{2,1,0:T(2,128)(2,1)} %reshape.186), calls=%async_computation.2 | async-start | bytes 524288 | tf_op jit(solution)/shard_map/all_to_all | solution.py:26
  86.5 0.8 copy-start.6
  86.5 0.8 copy-start.10
  87.5 7.1 %copy-start.8 = (bf16[8,1024]{1,0:T(8,128)(2,1)S(1)}, bf16[8,1024]{1,0:T(8,128)(2,1)}, u32[]{:S(2)}) copy-start(bf16[8,1024]{1,0:T(8,128)(2,1)} %param.19) | copy-start | bytes 49156
  87.8 12.9 %copy-start.2 = (f32[1024]{0:T(1024)S(1)}, f32[1024]{0:T(1024)}, u32[]{:S(2)}) copy-start(f32[1024]{0:T(1024)} %param.20) | copy-start | bytes 12292
  87.8 12.9 %copy-start.3 = (f32[1024]{0:T(1024)S(1)}, f32[1024]{0:T(1024)}, u32[]{:S(2)}) copy-start(f32[1024]{0:T(1024)} %param.22) | copy-start | bytes 12292
  89.0 11.7 %all-to-all-start.3 = ((f32[16,4,1152]{2,1,0:T(4,128)}), f32[16,4,1152]{2,1,0:T(4,128)S(1)}, u32[]{:S(2)}, u32[]{:S(2)}) async-start(f32[16,4,1152]{2,1,0:T(4,128)} %concatenate.22), calls=%async_computation.3 | async-start | bytes 589824 | tf_op jit(solution)/shard_map/all_to_all | solution.py:26
  100.7 1.6 copy-start.1
  107.0 18.9 %collective-permute-start.4 = (bf16[8,64,1280]{2,1,0:T(8,128)(2,1)}, bf16[8,64,1280]{2,1,0:T(8,128)(2,1)}, u32[]{:S(2)}, u32[]{:S(2)}) collective-permute-start(bf16[8,64,1280]{2,1,0:T(8,128)(2,1)} %get-tuple-element.19), channel_id=1, source_target_pairs={{0,1},{1,0},{2,3},{3,2},{4,5},{5,4},{6,7},{7,6},{8,9},{9,8},{10,11... | collective-permute-start | bytes 3932168 | tf_op jit(solution)/shard_map/ppermute | solution.py:257
  119.1 20.0 %all-to-all-start.5 = ((bf16[4,64,768]{2,1,0:T(8,128)(2,1)}), bf16[4,64,768]{2,1,0:T(8,128)(2,1)S(1)}, u32[]{:S(2)}, u32[]{:S(2)}) async-start(bf16[4,64,768]{2,1,0:T(8,128)(2,1)} %pad_maximum_fusion.1), calls=%async_computation.5 | async-start | bytes 786432 | tf_op jit(solution)/shard_map/all_to_all | solution.py:26
  139.1 20.4 %all-to-all-start.6 = ((bf16[8,64,1280]{2,1,0:T(8,128)(2,1)}), bf16[8,64,1280]{2,1,0:T(8,128)(2,1)S(1)}, u32[]{:S(2)}, u32[]{:S(2)}) async-start(bf16[8,64,1280]{2,1,0:T(8,128)(2,1)} %add_convert_fusion), calls=%async_computation.6 | async-start | bytes 2621440 | tf_op jit(solution)/shard_map/all_to_all | solution.py:26
  160.4 14.2 %all-to-all-start.7 = ((bf16[8,72,256]{2,1,0:T(8,128)(2,1)}), bf16[8,72,256]{2,1,0:T(8,128)(2,1)S(1)}, u32[]{:S(2)}, u32[]{:S(2)}) async-start(bf16[8,72,256]{2,1,0:T(8,128)(2,1)} %pad_maximum_fusion.2), calls=%async_computation.7 | async-start | bytes 589824 | tf_op jit(solution)/shard_map/all_to_all | solution.py:26

commit v3 on v2

--- a/solution.py
+++ b/solution.py
@@ -30,18 +30,17 @@
     return exchange(jnp.broadcast_to(block[None], (count,) + block.shape), axes)
 
 
-def from_others(block, axis, count):
-    return [
-        lax.ppermute(block, axis, [(i, (i - k) % count) for i in range(count)])
-        for k in range(1, count)
-    ]
+def from_further(block, axis, step):
+    count = PARTS[axis]
+    return lax.ppermute(block, axis, [(i, (i - step) % count) for i in range(count)])
 
 
 def finish_body(blocks_ref, first_ref, output_ref, hidden_ref):
     n_zh, n_y = PARTS["zh"], PARTS["y"]
     for y in range(n_y):
+        row = 256 * (y % 2) + 64 * (y // 2)
         for zh in range(n_zh):
-            first_ref[64 * y : 64 * (y + 1), 256 * zh : 256 * (zh + 1)] = blocks_ref[
+            first_ref[row : row + 64, 256 * zh : 256 * (zh + 1)] = blocks_ref[
                 n_y * zh + y, :64, :
             ].astype(f32)
     extra = blocks_ref[:, 64:80, :].astype(f32)
@@ -121,8 +120,10 @@
     row_sum = jnp.sum(first_grad.reshape(pairs // (2 * own), 2 * own, hidden), axis=0)
     row_grad = (row_sum[:own] + row_sum[own:]) * scale
     row_grad = row_grad.astype(bf16)
-    for t in range(n_t):
-        row_ref[t] = row_grad
+    cols = row_ref.shape[2]
+    for i in range(row_ref.shape[0]):
+        at = i // n_t * cols
+        row_ref[i] = row_grad[:, at : at + cols]
 
 
 def weights_body(core_ref, act_first_ref, second_grad_ref, act_second_ref, out_cot_ref, mine_ref, other_ref):
@@ -178,27 +179,35 @@
     targets = jnp.broadcast_to(own_labels[:, :, None], (own, classes, idx)).reshape(own, reads)
     targets = jnp.pad(targets, ((0, 0), (0, 256 - reads)))
     att = spread(attention, "y", n_y).reshape(n_y * rows, width)
+    half = width // 2
+    ahead, behind = from_further(out_proj, "zh", 1), from_further(out_proj, "zh", -1)
+    opposite = [from_further(ahead[:half], "zh", 1), from_further(behind[half:], "zh", -1)]
     part = jnp.zeros((n_zh, cols, n_y * rows), bf16)
-    for k, proj in enumerate([out_proj] + from_others(out_proj, "zh", n_zh)):
-        one = contract(proj, att, 0, 1).astype(bf16)
-        part = lax.dynamic_update_index_in_dim(part, one, (zh + k) % n_zh, 0)
+    for k, proj in ((0, out_proj), (1, ahead), (3, behind), (2, opposite)):
+        if k == 2:
+            one = contract(proj[0], att[:, :half], 0, 1) + contract(proj[1], att[:, half:], 0, 1)
+        else:
+            one = contract(proj, att, 0, 1)
+        part = lax.dynamic_update_index_in_dim(part, one.astype(bf16), (zh + k) % n_zh, 0)
     part = part.reshape(n_zh * 2, 2, quarter, n_y * rows)
     mine = lax.dynamic_index_in_dim(part, c, 1, keepdims=False)
     other = lax.dynamic_index_in_dim(part, 1 - c, 1, keepdims=False)
     swapped = lax.ppermute(other, "c", [(0, 1), (1, 0)])
     pair = (mine.astype(f32) + swapped.astype(f32)).astype(bf16)
     branch = jnp.sum(exchange(pair, ("x", "zl")).astype(f32), axis=0).astype(bf16)
-    branch = branch.reshape(quarter, n_y, rows).transpose(1, 0, 2)
-    slot = (jnp.arange(4) == y // 2)[None, :, None, None]
-    branch = jnp.where(slot, branch[:, None], jnp.zeros((), bf16))
-    branch = exchange(branch.reshape(n_y * 4, quarter, rows), ("y", "zl", "c"))
-    branch = branch.reshape(n_y, 4 * quarter, rows)
-    branch = lax.dynamic_slice_in_dim(branch, 2 * (2 * zl + c), 2, 0).reshape(width, rows)
-
-    state = residual.astype(f32).T + branch.astype(f32)
+    branch = exchange(branch.reshape(quarter, n_y, rows).transpose(1, 0, 2), "y")
+    branch = exchange(branch.reshape(4, 2, quarter, rows), ("zl", "c")).reshape(width, rows)
+
+    def reordered(values):
+        values = values.reshape((2, 4, quarter) + values.shape[1:])
+        return jnp.swapaxes(values, 0, 1).reshape((width,) + values.shape[3:])
+
+    w_first, norm_gain = reordered(w_first), reordered(norm_gain)
+    state = reordered(residual.astype(f32).T) + branch.astype(f32)
     square_sum = jnp.sum(state * state, axis=0)
     gained = (state * norm_gain[:, None]).astype(bf16).T
     first = jnp.dot(gained, w_first, preferred_element_type=f32)
+    gained_all = lax.all_gather(gained, "zh", axis=0, tiled=True)
     own_draws = samples // n_t * idx
     extra = jnp.concatenate(
         [
@@ -213,10 +222,10 @@
 
     pairs = own * samples
     by_pair = jax.ShapeDtypeStruct((pairs, hidden), bf16)
-    row_grad, act_first, second_grad, act_second, out_cot = pl.pallas_call(
+    row_blocks, act_first, second_grad, act_second, out_cot = pl.pallas_call(
         epinet_body,
         out_shape=(
-            jax.ShapeDtypeStruct((n_t, own, hidden), bf16),
+            jax.ShapeDtypeStruct((n_zh * n_t, own, cols), bf16),
             by_pair,
             by_pair,
             by_pair,
@@ -238,10 +247,7 @@
         same,
     )
 
-    row_blocks = exchange(row_grad, TENSOR).reshape(rows, n_zh, cols).transpose(1, 0, 2)
-    both = jnp.broadcast_to(gained[None], (n_zh, rows, width))
-    both = exchange(jnp.concatenate([both, row_blocks], axis=2), "zh").reshape(n_zh * rows, -1)
-    gained_all, row_blocks = both[:, :width], both[:, width:]
+    row_blocks = exchange(row_blocks, ("zh",) + TENSOR).reshape(n_zh * rows, cols)
 
     half = jax.ShapeDtypeStruct((n_t // 2, hidden // n_t, hidden + 256), bf16)
     vmem = pl.BlockSpec(memory_space=pltpu.VMEM)

time: 223 us -> 217 us (0.973)
  waiting for transfers between devices: 77 us -> 51.6 us
  starting transfers between devices: 65.1 us -> 76.4 us
  blocking collectives: 53 us -> 63.7 us
    all_gather x0 -> x1, blocking collectives: none -> 25.2 us  [shards(): gained_all = lax.all_gather(gained, 'zh', axis=0, tiled=True)]
    all_to_all x7 -> x8, waiting for transfers between devices: 60.2 us -> 41.8 us  [exchange(): return lax.all_to_all(blocks, axes, 0, 0, tiled=True)]
    all_to_all x2 -> x1, blocking collectives: 53 us -> 38.6 us  [exchange(): return lax.all_to_all(blocks, axes, 0, 0, tiled=True)]
    ppermute x3 -> x4, starting transfers between devices: 17.7 us -> 25.4 us  [from_further(): lax.ppermute(block, axis, [(i, (i - step) % count) for i in range(count)])]
    ppermute x3 -> x4, waiting for transfers between devices: 14.9 us -> 7.9 us  [from_further(): lax.ppermute(block, axis, [(i, (i - step) % count) for i in range(count)])]
    all_to_all x7 -> x8, starting transfers between devices: 43.6 us -> 47.1 us  [exchange(): return lax.all_to_all(blocks, axes, 0, 0, tiled=True)]
  transfers between devices with their start and end apart: 12 -> 14, of which waited for: 8 -> 10; matrix products, arithmetic and copies ran while one was open for 3% -> 3% of each run, Pallas kernels for 0% -> 0%
where the time goes in v3:
time: 217 us; the launch traced here: 214 us
  starting transfers between devices  76.4 us (35%)
  blocking collectives  63.7 us (29%)
  waiting for transfers between devices  51.6 us (24%)
  local copies, waits for them, and re-layouts  8.11 us (4%)
  Pallas kernels  5.84 us (3%)
  other arithmetic  5 us (2%)
  matrix products  2.28 us (1%)
    all_to_all x8, starting transfers between devices, exchange(): return lax.all_to_all(blocks, axes, 0, 0, tiled=True)  47.1 us
    all_to_all x8, waiting for transfers between devices, exchange(): return lax.all_to_all(blocks, axes, 0, 0, tiled=True)  41.8 us
    all_to_all x1, blocking collectives, exchange(): return lax.all_to_all(blocks, axes, 0, 0, tiled=True)  38.6 us
    ppermute x4, starting transfers between devices, from_further(): lax.ppermute(block, axis, [(i, (i - step) % count) for i in range(count)])  25.4 us
    all_gather x1, blocking collectives, shards(): gained_all = lax.all_gather(gained, 'zh', axis=0, tiled=True)  25.2 us
    ppermute x4, waiting for transfers between devices, from_further(): lax.ppermute(block, axis, [(i, (i - step) % count) for i in range(count)])  7.9 us
  transfers between devices with their start and end apart: 14, of which 10 were waited for; matrix products, arithmetic and copies ran while one was open for 3% of the time, Pallas kernels for 0%

profile of v3, /device:TPU:6, one launch (start us, length us, event | category | flops | bytes accessed | tf_op | source)
XLA Modules:
  0.0 214.2 jit_solution(555333178303690654)
XLA Ops:
  0.7 1.7 broadcast_in_dim.50
  2.4 7.1 %all-to-all-start = ((bf16[8,64,512]{2,1,0:T(8,128)(2,1)}), bf16[8,64,512]{2,1,0:T(8,128)(2,1)S(1)}, u32[]{:S(2)}, u32[]{:S(2)}) async-start(bf16[8,64,512]{2,1,0:T(8,128)(2,1)} %broadcast_in_dim.50), calls=%async_computation | async-start | bytes 1048576 | tf_op jit(solution)/shard_map/all_to_all | solution.py:26
  9.5 6.1 %collective-permute-start.1 = (bf16[512,256]{1,0:T(8,128)(2,1)S(1)}, bf16[512,256]{1,0:T(8,128)(2,1)S(1)}, u32[]{:S(2)}, u32[]{:S(2)}) collective-permute-start(bf16[512,256]{1,0:T(8,128)(2,1)S(1)} %copy-done.6), channel_id=1, source_target_pairs={{0,128},{128,256},{256,384},{384,0},{1,129},{129,257},{257,385},{3... | collective-permute-start | bytes 786440 | tf_op jit(solution)/shard_map/ppermute | solution.py:35
  15.6 6.8 %collective-permute-start = (bf16[512,256]{1,0:T(8,128)(2,1)S(1)}, bf16[512,256]{1,0:T(8,128)(2,1)S(1)}, u32[]{:S(2)}, u32[]{:S(2)}) collective-permute-start(bf16[512,256]{1,0:T(8,128)(2,1)S(1)} %copy-done.6), channel_id=1, source_target_pairs={{0,384},{128,0},{256,128},{384,256},{1,385},{129,1},{257,129},{385... | collective-permute-start | bytes 786440 | tf_op jit(solution)/shard_map/ppermute | solution.py:35
  22.4 4.2 %collective-permute-done.1 = bf16[512,256]{1,0:T(8,128)(2,1)S(1)} collective-permute-done((bf16[512,256]{1,0:T(8,128)(2,1)S(1)}, bf16[512,256]{1,0:T(8,128)(2,1)S(1)}, u32[]{:S(2)}, u32[]{:S(2)}) %collective-permute-start.1) | collective-permute-done | bytes 262176 | tf_op jit(solution)/shard_map/ppermute | solution.py:35
  26.6 7.2 %collective-permute-start.3 = (bf16[256,256]{1,0:T(8,128)(2,1)S(1)}, bf16[256,256]{1,0:T(8,128)(2,1)S(1)}, u32[]{:S(2)}, u32[]{:S(2)}) collective-permute-start(bf16[256,256]{1,0:T(8,128)(2,1)S(1)} %slice.26), channel_id=1, source_target_pairs={{0,128},{128,256},{256,384},{384,0},{1,129},{129,257},{257,385},{3... | collective-permute-start | bytes 393224 | tf_op jit(solution)/shard_map/ppermute | solution.py:35
  33.8 5.4 %collective-permute-start.2 = (bf16[256,256]{1,0:T(8,128)(2,1)S(1)}, bf16[256,256]{1,0:T(8,128)(2,1)S(1)}, u32[]{:S(2)}, u32[]{:S(2)}) collective-permute-start(bf16[256,256]{1,0:T(8,128)(2,1)S(1)} %slice.24), channel_id=1, source_target_pairs={{0,384},{128,0},{256,128},{384,256},{1,385},{129,1},{257,129},{385... | collective-permute-start | bytes 393224 | tf_op jit(solution)/shard_map/ppermute | solution.py:35
  39.3 0.4 fusion.4
  39.7 0.4 fusion.6
  40.0 0.4 fusion.8
  40.4 1.1 collective-permute-done.3
  41.5 0.3 fusion.12
  41.8 2.6 %collective-permute-done.2 = bf16[256,256]{1,0:T(8,128)(2,1)S(1)} collective-permute-done((bf16[256,256]{1,0:T(8,128)(2,1)S(1)}, bf16[256,256]{1,0:T(8,128)(2,1)S(1)}, u32[]{:S(2)}, u32[]{:S(2)}) %collective-permute-start.2) | collective-permute-done | bytes 131104 | tf_op jit(solution)/shard_map/ppermute | solution.py:35
  44.4 0.3 fusion.2
  44.7 1.9 collective-permute-start.4
  46.7 1.9 collective-permute-done.4
  48.5 0.9 fusion.9
  49.5 6.6 %all-to-all-start.1 = ((bf16[8,64,512]{2,1,0:T(8,128)(2,1)}), bf16[8,64,512]{2,1,0:T(8,128)(2,1)S(1)}, u32[]{:S(2)}, u32[]{:S(2)}) async-start(bf16[8,64,512]{2,1,0:T(8,128)(2,1)} %fusion.9), calls=%async_computation.1 | async-start | bytes 1048576 | tf_op jit(solution)/shard_map/all_to_all | solution.py:26
  56.0 0.2 reshape.195
  56.2 0.1 copy.74
  56.4 0.1 copy.83
  56.6 0.1 reshape.194
  56.7 7.3 %all-to-all-done.1 = bf16[8,64,512]{2,1,0:T(8,128)(2,1)S(1)} async-done(((bf16[8,64,512]{2,1,0:T(8,128)(2,1)}), bf16[8,64,512]{2,1,0:T(8,128)(2,1)S(1)}, u32[]{:S(2)}, u32[]{:S(2)}) %all-to-all-start.1) | async-done | bytes 524320 | tf_op jit(solution)/shard_map/all_to_all | solution.py:26
  64.1 0.1 reshape.180
  64.3 0.8 reshape.197
  65.1 6.9 %all-to-all-start.2 = ((bf16[8,2,2048]{2,1,0:T(2,128)(2,1)}), bf16[8,2,2048]{2,1,0:T(2,128)(2,1)S(1)}, u32[]{:S(2)}, u32[]{:S(2)}) async-start(bf16[8,2,2048]{2,1,0:T(2,128)(2,1)} %reshape.197), calls=%async_computation.2 | async-start | bytes 131072 | tf_op jit(solution)/shard_map/all_to_all | solution.py:26
  71.9 8.4 %all-to-all-done.2 = bf16[8,2,2048]{2,1,0:T(2,128)(2,1)S(1)} async-done(((bf16[8,2,2048]{2,1,0:T(2,128)(2,1)}), bf16[8,2,2048]{2,1,0:T(2,128)(2,1)S(1)}, u32[]{:S(2)}, u32[]{:S(2)}) %all-to-all-start.2) | async-done | bytes 65568 | tf_op jit(solution)/shard_map/all_to_all | solution.py:26
  80.3 0.1 reshape.198
  80.4 0.1 copy.76
  80.6 0.8 reshape.199
  81.4 3.3 %all-to-all-start.3 = ((bf16[4,2,4096]{2,1,0:T(2,128)(2,1)}), bf16[4,2,4096]{2,1,0:T(2,128)(2,1)S(1)}, u32[]{:S(2)}, u32[]{:S(2)}) async-start(bf16[4,2,4096]{2,1,0:T(2,128)(2,1)} %reshape.199), calls=%async_computation.3 | async-start | bytes 131072 | tf_op jit(solution)/shard_map/all_to_all | solution.py:26
  84.8 0.1 copy.93
  84.9 0.1 reshape.184
  85.0 0.2 copy.85
  85.4 3.4 %all-to-all-done.3 = bf16[4,2,4096]{2,1,0:T(2,128)(2,1)S(1)} async-done(((bf16[4,2,4096]{2,1,0:T(2,128)(2,1)}), bf16[4,2,4096]{2,1,0:T(2,128)(2,1)S(1)}, u32[]{:S(2)}, u32[]{:S(2)}) %all-to-all-start.3) | async-done | bytes 65568 | tf_op jit(solution)/shard_map/all_to_all | solution.py:26
  88.8 0.1 reshape.200
  88.9 0.1 copy.77
  89.0 0.1 multiply_reduce_fusion
  89.2 0.4 convolution_bitcast_fusion
  89.7 0.2 concatenate.23
  89.9 0.9 concatenate.19
  90.8 5.8 %all-to-all-start.4 = ((f32[16,4,1152]{2,1,0:T(4,128)}), f32[16,4,1152]{2,1,0:T(4,128)S(1)}, u32[]{:S(2)}, u32[]{:S(2)}) async-start(f32[16,4,1152]{2,1,0:T(4,128)} %concatenate.19), calls=%async_computation.4 | async-start | bytes 589824 | tf_op jit(solution)/shard_map/all_to_all | solution.py:26
  96.6 0.1 compare_convert_fusion.same_ref
  96.7 6.0 %all-to-all-done.4.first_ref = f32[16,4,1152]{2,1,0:T(4,128)S(1)} async-done(((f32[16,4,1152]{2,1,0:T(4,128)}), f32[16,4,1152]{2,1,0:T(4,128)S(1)}, u32[]{:S(2)}, u32[]{:S(2)}) %all-to-all-start.4) | async-done | bytes 294944 | tf_op jit(solution)/shard_map/all_to_all | solution.py:26
  102.7 3.4 %shard_map.139 = (bf16[64,4,256]{2,1,0:T(4,128)(2,1)}, bf16[256,1024]{1,0:T(8,128)(2,1)S(1)}, bf16[256,1024]{1,0:T(8,128)(2,1)S(1)}, bf16[256,1024]{1,0:T(8,128)(2,1)S(1)}, bf16[256,256]{1,0:T(8,128)(2,1)S(1)}) custom-call(f32[16,4,1152]{2,1,0:T(4,128)S(1)} %all-to-all-done.4.first_ref, bf16[8,1280]{1,0:T(8,128)(2,1)S(1)} %pad_maximum_fusion.2.index_ref, ...), custom_call_target="tpu_custom_call" | custom-call | flops 2000000000 | bytes 8388608 | tf_op jit(solution)/shard_map/pallas_call | solution.py:225
  106.1 0.9 shard_map.140
  107.1 1.9 collective-permute-start.5
  109.0 9.0 %all-to-all-start.5 = ((bf16[64,4,256]{2,1,0:T(4,128)(2,1)}), bf16[64,4,256]{2,1,0:T(4,128)(2,1)S(1)}, u32[]{:S(2)}, u32[]{:S(2)}) async-start(bf16[64,4,256]{2,1,0:T(4,128)(2,1)} %get-tuple-element.13), calls=%async_computation.5 | async-start | bytes 262144 | tf_op jit(solution)/shard_map/all_to_all | solution.py:26
  118.0 2.7 %add_convert_fusion = bf16[8,64,1280]{2,1,0:T(8,128)(2,1)} fusion(bf16[8,64,1280]{2,1,0:T(8,128)(2,1)} %collective-permute-done.5, bf16[8,64,1280]{2,1,0:T(8,128)(2,1)S(1)} %get-tuple-element.18), kind=kLoop, calls=%fused_computation | loop fusion | flops 2621440 | bytes 3932160 | tf_op jit(solution)/shard_map/convert_element_type | solution.py:264
  120.7 6.6 %all-to-all-done.5 = bf16[64,4,256]{2,1,0:T(4,128)(2,1)S(1)} async-done(((bf16[64,4,256]{2,1,0:T(4,128)(2,1)}), bf16[64,4,256]{2,1,0:T(4,128)(2,1)S(1)}, u32[]{:S(2)}, u32[]{:S(2)}) %all-to-all-start.5) | async-done | bytes 131104 | tf_op jit(solution)/shard_map/all_to_all | solution.py:26
  127.3 5.1 %all-to-all-start.6 = ((bf16[8,64,1280]{2,1,0:T(8,128)(2,1)}), bf16[8,64,1280]{2,1,0:T(8,128)(2,1)S(1)}, u32[]{:S(2)}, u32[]{:S(2)}) async-start(bf16[8,64,1280]{2,1,0:T(8,128)(2,1)} %add_convert_fusion), calls=%async_computation.6 | async-start | bytes 2621440 | tf_op jit(solution)/shard_map/all_to_all | solution.py:26
  132.5 0.1 copy.92
  132.7 25.2 %all_gather.3 = bf16[256,512]{1,0:T(8,128)(2,1)S(1)} all-gather(bf16[64,512]{1,0:T(8,128)(2,1)S(1)} %fusion.16), channel_id=1, replica_groups=mesh['zh'=4,'y'=8,'x'=4,'zl'=2,'c'=2] {'zh'}, dimensions={0}, use_global_device_ids=true | all-gather | bytes 327680 | tf_op jit(solution)/shard_map/all_gather | solution.py:210
  157.9 0.3 convolution_convert_fusion
  158.1 0.2 reduce_sum.47
  158.4 0.7 pad_maximum_fusion.1
  159.1 3.4 %all-to-all-start.7 = ((bf16[8,72,256]{2,1,0:T(8,128)(2,1)}), bf16[8,72,256]{2,1,0:T(8,128)(2,1)S(1)}, u32[]{:S(2)}, u32[]{:S(2)}) async-start(bf16[8,72,256]{2,1,0:T(8,128)(2,1)} %pad_maximum_fusion.1), calls=%async_computation.7 | async-start | bytes 589824 | tf_op jit(solution)/shard_map/all_to_all | solution.py:26
  162.5 0.2 copy.87
  162.7 0.1 copy.88
  162.8 0.2 reshape.190
  163.0 10.2 %all-to-all-done.7 = bf16[8,72,256]{2,1,0:T(8,128)(2,1)S(1)} async-done(((bf16[8,72,256]{2,1,0:T(8,128)(2,1)}), bf16[8,72,256]{2,1,0:T(8,128)(2,1)S(1)}, u32[]{:S(2)}, u32[]{:S(2)}) %all-to-all-start.7) | async-done | bytes 294944 | tf_op jit(solution)/shard_map/all_to_all | solution.py:26
  173.5 38.6 %all_to_all.45.blocks_ref = bf16[32,80,256]{2,1,0:T(8,128)(2,1)S(1)} all-to-all(bf16[32,80,256]{2,1,0:T(8,128)(2,1)S(1)} %pad_maximum_fusion), channel_id=1, replica_groups=mesh['zh'=4,'y'=8,'x'=4,'zl'=2,'c'=2] {'zh','y'}, dimensions={0} | all-to-all | bytes 2621440 | tf_op jit(solution)/shard_map/all_to_all | solution.py:26
  212.0 1.5 shard_map.141
  213.6 0.6 copy.99
  (56 shorter events, 1.2 us)
Async XLA Ops:
  0.6 84.0 %copy-start = (s32[64,25]{0,1:T(8,128)S(1)}, s32[64,25]{0,1:T(8,128)}, u32[]{:S(2)}) copy-start(s32[64,25]{0,1:T(8,128)} %param.17) | copy-start | bytes 19204
  0.6 8.8 %copy-start.6 = (bf16[512,256]{1,0:T(8,128)(2,1)S(1)}, bf16[512,256]{1,0:T(8,128)(2,1)}, u32[]{:S(2)}) copy-start(bf16[512,256]{1,0:T(8,128)(2,1)} %param.14) | copy-start | bytes 786436
  2.4 36.8 %all-to-all-start = ((bf16[8,64,512]{2,1,0:T(8,128)(2,1)}), bf16[8,64,512]{2,1,0:T(8,128)(2,1)S(1)}, u32[]{:S(2)}, u32[]{:S(2)}) async-start(bf16[8,64,512]{2,1,0:T(8,128)(2,1)} %broadcast_in_dim.50), calls=%async_computation | async-start | bytes 1048576 | tf_op jit(solution)/shard_map/all_to_all | solution.py:26
  9.5 17.1 %collective-permute-start.1 = (bf16[512,256]{1,0:T(8,128)(2,1)S(1)}, bf16[512,256]{1,0:T(8,128)(2,1)S(1)}, u32[]{:S(2)}, u32[]{:S(2)}) collective-permute-start(bf16[512,256]{1,0:T(8,128)(2,1)S(1)} %copy-done.6), channel_id=1, source_target_pairs={{0,128},{128,256},{256,384},{384,0},{1,129},{129,257},{257,385},{3... | collective-permute-start | bytes 786440 | tf_op jit(solution)/shard_map/ppermute | solution.py:35
  15.6 18.2 %collective-permute-start = (bf16[512,256]{1,0:T(8,128)(2,1)S(1)}, bf16[512,256]{1,0:T(8,128)(2,1)S(1)}, u32[]{:S(2)}, u32[]{:S(2)}) collective-permute-start(bf16[512,256]{1,0:T(8,128)(2,1)S(1)} %copy-done.6), channel_id=1, source_target_pairs={{0,384},{128,0},{256,128},{384,256},{1,385},{129,1},{257,129},{385... | collective-permute-start | bytes 786440 | tf_op jit(solution)/shard_map/ppermute | solution.py:35
  26.6 14.9 %collective-permute-start.3 = (bf16[256,256]{1,0:T(8,128)(2,1)S(1)}, bf16[256,256]{1,0:T(8,128)(2,1)S(1)}, u32[]{:S(2)}, u32[]{:S(2)}) collective-permute-start(bf16[256,256]{1,0:T(8,128)(2,1)S(1)} %slice.26), channel_id=1, source_target_pairs={{0,128},{128,256},{256,384},{384,0},{1,129},{129,257},{257,385},{3... | collective-permute-start | bytes 393224 | tf_op jit(solution)/shard_map/ppermute | solution.py:35
  33.8 10.6 %collective-permute-start.2 = (bf16[256,256]{1,0:T(8,128)(2,1)S(1)}, bf16[256,256]{1,0:T(8,128)(2,1)S(1)}, u32[]{:S(2)}, u32[]{:S(2)}) collective-permute-start(bf16[256,256]{1,0:T(8,128)(2,1)S(1)} %slice.24), channel_id=1, source_target_pairs={{0,384},{128,0},{256,128},{384,256},{1,385},{129,1},{257,129},{385... | collective-permute-start | bytes 393224 | tf_op jit(solution)/shard_map/ppermute | solution.py:35
  44.7 3.8 %collective-permute-start.4 = (bf16[8,64,512]{2,1,0:T(8,128)(2,1)S(1)}, bf16[8,64,512]{2,1,0:T(8,128)(2,1)S(1)}, u32[]{:S(2)}, u32[]{:S(2)}) collective-permute-start(bf16[8,64,512]{2,1,0:T(8,128)(2,1)S(1)} %dynamic-slice_bitcast_fusion), channel_id=1, source_target_pairs={{0,1},{1,0},{2,3},{3,2},{4,5},{5,4},{6,7},{7,6},{8,9},{9,8},{10,11... | collective-permute-start | bytes 1572872 | tf_op jit(solution)/shard_map/ppermute | solution.py:195
  46.6 9.4 %copy-start.7 = (bf16[64,512]{1,0:T(8,128)(2,1)S(1)}, bf16[64,512]{1,0:T(8,128)(2,1)}, u32[]{:S(2)}) copy-start(bf16[64,512]{1,0:T(8,128)(2,1)} %param.12) | copy-start | bytes 196612
  49.5 6.9 %copy-start.10 = (f32[512]{0:T(512)S(1)}, f32[512]{0:T(512)}, u32[]{:S(2)}) copy-start(f32[512]{0:T(512)} %param.15) | copy-start | bytes 6148
  49.5 7.0 %copy-start.9 = (bf16[64,4,8]{0,2,1:T(8,128)(2,1)S(1)}, bf16[64,4,8]{0,2,1:T(8,128)(2,1)}, u32[]{:S(2)}) copy-start(bf16[64,4,8]{0,2,1:T(8,128)(2,1)} %param.16) | copy-start | bytes 12292
  49.5 14.6 %all-to-all-start.1 = ((bf16[8,64,512]{2,1,0:T(8,128)(2,1)}), bf16[8,64,512]{2,1,0:T(8,128)(2,1)S(1)}, u32[]{:S(2)}, u32[]{:S(2)}) async-start(bf16[8,64,512]{2,1,0:T(8,128)(2,1)} %fusion.9), calls=%async_computation.1 | async-start | bytes 1048576 | tf_op jit(solution)/shard_map/all_to_all | solution.py:26
  56.6 28.5 %copy-start.5 = (bf16[1024,200]{0,1:T(8,128)(2,1)S(1)}, bf16[1024,200]{0,1:T(8,128)(2,1)}, u32[]{:S(2)}) copy-start(bf16[1024,200]{0,1:T(8,128)(2,1)} %param.23) | copy-start | bytes 1228804
  65.1 15.2 %all-to-all-start.2 = ((bf16[8,2,2048]{2,1,0:T(2,128)(2,1)}), bf16[8,2,2048]{2,1,0:T(2,128)(2,1)S(1)}, u32[]{:S(2)}, u32[]{:S(2)}) async-start(bf16[8,2,2048]{2,1,0:T(2,128)(2,1)} %reshape.197), calls=%async_computation.2 | async-start | bytes 131072 | tf_op jit(solution)/shard_map/all_to_all | solution.py:26
  81.4 7.4 %all-to-all-start.3 = ((bf16[4,2,4096]{2,1,0:T(2,128)(2,1)}), bf16[4,2,4096]{2,1,0:T(2,128)(2,1)S(1)}, u32[]{:S(2)}, u32[]{:S(2)}) async-start(bf16[4,2,4096]{2,1,0:T(2,128)(2,1)} %reshape.199), calls=%async_computation.3 | async-start | bytes 131072 | tf_op jit(solution)/shard_map/all_to_all | solution.py:26
  85.3 3.9 %copy-start.4 = (bf16[512,1024]{1,0:T(8,128)(2,1)S(1)}, bf16[512,1024]{1,0:T(8,128)(2,1)}, u32[]{:S(2)}) copy-start(bf16[512,1024]{1,0:T(8,128)(2,1)} %param.18) | copy-start | bytes 3145732
  89.1 7.4 %copy-start.8 = (bf16[8,1024]{1,0:T(8,128)(2,1)S(1)}, bf16[8,1024]{1,0:T(8,128)(2,1)}, u32[]{:S(2)}) copy-start(bf16[8,1024]{1,0:T(8,128)(2,1)} %param.19) | copy-start | bytes 49156
  89.6 13.1 %copy-start.1 = (bf16[1024,1024]{1,0:T(8,128)(2,1)S(1)}, bf16[1024,1024]{1,0:T(8,128)(2,1)}, u32[]{:S(2)}) copy-start(bf16[1024,1024]{1,0:T(8,128)(2,1)} %w_hidden_ref.1) | copy-start | bytes 6291460
  89.6 13.1 %copy-start.2 = (f32[1024]{0:T(1024)S(1)}, f32[1024]{0:T(1024)}, u32[]{:S(2)}) copy-start(f32[1024]{0:T(1024)} %param.20) | copy-start | bytes 12292
  89.6 13.1 %copy-start.3 = (f32[1024]{0:T(1024)S(1)}, f32[1024]{0:T(1024)}, u32[]{:S(2)}) copy-start(f32[1024]{0:T(1024)} %param.22) | copy-start | bytes 12292
  90.8 11.9 %all-to-all-start.4 = ((f32[16,4,1152]{2,1,0:T(4,128)}), f32[16,4,1152]{2,1,0:T(4,128)S(1)}, u32[]{:S(2)}, u32[]{:S(2)}) async-start(f32[16,4,1152]{2,1,0:T(4,128)} %concatenate.19), calls=%async_computation.4 | async-start | bytes 589824 | tf_op jit(solution)/shard_map/all_to_all | solution.py:26
  107.1 11.0 %collective-permute-start.5 = (bf16[8,64,1280]{2,1,0:T(8,128)(2,1)S(1)}, bf16[8,64,1280]{2,1,0:T(8,128)(2,1)}, u32[]{:S(2)}, u32[]{:S(2)}) collective-permute-start(bf16[8,64,1280]{2,1,0:T(8,128)(2,1)S(1)} %get-tuple-element.19), channel_id=1, source_target_pairs={{0,1},{1,0},{2,3},{3,2},{4,5},{5,4},{6,7},{7,6},{8,9},{9,8},{10,11... | collective-permute-start | bytes 3932168 | tf_op jit(solution)/shard_map/ppermute | solution.py:263
  109.0 18.3 %all-to-all-start.5 = ((bf16[64,4,256]{2,1,0:T(4,128)(2,1)}), bf16[64,4,256]{2,1,0:T(4,128)(2,1)S(1)}, u32[]{:S(2)}, u32[]{:S(2)}) async-start(bf16[64,4,256]{2,1,0:T(4,128)(2,1)} %get-tuple-element.13), calls=%async_computation.5 | async-start | bytes 262144 | tf_op jit(solution)/shard_map/all_to_all | solution.py:26
  127.3 30.8 %all-to-all-start.6 = ((bf16[8,64,1280]{2,1,0:T(8,128)(2,1)}), bf16[8,64,1280]{2,1,0:T(8,128)(2,1)S(1)}, u32[]{:S(2)}, u32[]{:S(2)}) async-start(bf16[8,64,1280]{2,1,0:T(8,128)(2,1)} %add_convert_fusion), calls=%async_computation.6 | async-start | bytes 2621440 | tf_op jit(solution)/shard_map/all_to_all | solution.py:26
  159.1 14.2 %all-to-all-start.7 = ((bf16[8,72,256]{2,1,0:T(8,128)(2,1)}), bf16[8,72,256]{2,1,0:T(8,128)(2,1)S(1)}, u32[]{:S(2)}, u32[]{:S(2)}) async-start(bf16[8,72,256]{2,1,0:T(8,128)(2,1)} %pad_maximum_fusion.1), calls=%async_computation.7 | async-start | bytes 589824 | tf_op jit(solution)/shard_map/all_to_all | solution.py:26

commit v4 on v3

--- a/solution.py
+++ b/solution.py
@@ -38,18 +38,50 @@
 def finish_body(blocks_ref, first_ref, output_ref, hidden_ref):
     n_zh, n_y = PARTS["zh"], PARTS["y"]
     for y in range(n_y):
-        row = 256 * (y % 2) + 64 * (y // 2)
-        for zh in range(n_zh):
-            first_ref[row : row + 64, 256 * zh : 256 * (zh + 1)] = blocks_ref[
-                n_y * zh + y, :64, :
-            ].astype(f32)
+        for p in range(2):
+            row = 256 * p + 64 * (y % 4) + 32 * (y // 4)
+            for zh in range(n_zh):
+                first_ref[row : row + 32, 256 * zh : 256 * (zh + 1)] = blocks_ref[
+                    n_y * zh + y, 32 * p : 32 * (p + 1), :
+                ].astype(f32)
     extra = blocks_ref[:, 64:80, :].astype(f32)
     for y in range(n_y):
         total = extra[y]
         for zh in range(1, n_zh):
             total = total + extra[n_y * zh + y]
         output_ref[8 * y : 8 * (y + 1), :] = total[:8, :200]
-    hidden_ref[...] = jnp.sum(extra, axis=0)[8:]
+    hidden = jnp.sum(extra, axis=0)[8:]
+    pieces = [hidden[:, :128], pltpu.roll(hidden[:, :128], 64, 1)]
+    pieces += [hidden[:, 128:], pltpu.roll(hidden[:, 128:], 64, 1)]
+    hidden_ref[...] = jnp.concatenate(pieces, axis=0)[:, :64]
+
+
+def branch_body(parts_ref, blocks_ref):
+    total = jnp.sum(parts_ref[...].astype(f32), axis=0)
+    left = lax.broadcasted_iota(jnp.int32, (32, 128), 1) < 64
+    for i in range(total.shape[1] // 128):
+        top, bottom = total[:32, 128 * i : 128 * (i + 1)], total[32:, 128 * i : 128 * (i + 1)]
+        even = jnp.where(left, top, pltpu.roll(bottom, 64, 1))
+        odd = jnp.where(left, pltpu.roll(top, 64, 1), bottom)
+        blocks_ref[2 * i] = even.astype(bf16)
+        blocks_ref[2 * i + 1] = odd.astype(bf16)
+
+
+def state_body(branch_ref, residual_ref, gain_ref, w_first_ref, extra_ref, first_ref, gained_ref):
+    state = residual_ref[...].astype(f32) + branch_ref[...].astype(f32)
+    square_sum = jnp.sum((state * state).T, axis=1, keepdims=True)
+    square_sum = square_sum[:64] + square_sum[64:]
+    gained = (state * gain_ref[...]).T
+    gained = jnp.concatenate([gained[:64], gained[64:]], axis=1).astype(bf16)
+    gained_ref[...] = gained
+    first = jnp.dot(gained, w_first_ref[...], preferred_element_type=f32)
+    extra = extra_ref[...]
+    lane = lax.broadcasted_iota(jnp.int32, extra.shape, 1)
+    extra = jnp.where(lane == 32, square_sum, extra)
+    own, width = first_ref.shape[1], first.shape[1]
+    for t in range(first_ref.shape[0]):
+        first_ref[t, :, :width] = first[own * t : own * (t + 1)]
+        first_ref[t, :, width:] = extra[own * t : own * (t + 1)]
 
 
 def epinet_body(
@@ -194,30 +226,32 @@
     other = lax.dynamic_index_in_dim(part, 1 - c, 1, keepdims=False)
     swapped = lax.ppermute(other, "c", [(0, 1), (1, 0)])
     pair = (mine.astype(f32) + swapped.astype(f32)).astype(bf16)
-    branch = jnp.sum(exchange(pair, ("x", "zl")).astype(f32), axis=0).astype(bf16)
-    branch = exchange(branch.reshape(quarter, n_y, rows).transpose(1, 0, 2), "y")
-    branch = exchange(branch.reshape(4, 2, quarter, rows), ("zl", "c")).reshape(width, rows)
-
-    def reordered(values):
-        values = values.reshape((2, 4, quarter) + values.shape[1:])
-        return jnp.swapaxes(values, 0, 1).reshape((width,) + values.shape[3:])
-
-    w_first, norm_gain = reordered(w_first), reordered(norm_gain)
-    state = reordered(residual.astype(f32).T) + branch.astype(f32)
-    square_sum = jnp.sum(state * state, axis=0)
-    gained = (state * norm_gain[:, None]).astype(bf16).T
-    first = jnp.dot(gained, w_first, preferred_element_type=f32)
+    branch = pl.pallas_call(
+        branch_body,
+        out_shape=jax.ShapeDtypeStruct((n_y, 32, 128), bf16),
+        compiler_params=pltpu.CompilerParams(vmem_limit_bytes=16 * 2**20),
+        cost_estimate=pl.CostEstimate(flops=2**18, bytes_accessed=2**19, transcendentals=0),
+    )(exchange(pair, ("x", "zl")))
+    branch = exchange(exchange(branch, "y").reshape(4, 64, 128), ("zl", "c")).reshape(256, 128)
+
+    parts = (2, 4, 2, 32)
+    residual = residual.reshape((rows,) + parts).transpose(2, 1, 4, 3, 0).reshape(256, 128)
+    gain = norm_gain.reshape(parts).transpose(1, 0, 3, 2)[..., None]
+    gain = jnp.broadcast_to(gain, gain.shape[:-1] + (rows,)).reshape(256, 128)
+    w_first = w_first.reshape(parts + (hidden,)).transpose(2, 1, 0, 3, 4).reshape(width, hidden)
+    own_draws = samples // n_t * idx
+    extra = index_draws.reshape(rows, own_draws).astype(f32)
+    extra = jnp.pad(extra, ((0, 0), (0, 128 - own_draws)))
+    first, gained = pl.pallas_call(
+        state_body,
+        out_shape=(
+            jax.ShapeDtypeStruct((n_t, own, hidden + 128), f32),
+            jax.ShapeDtypeStruct((rows, width), bf16),
+        ),
+        compiler_params=pltpu.CompilerParams(vmem_limit_bytes=16 * 2**20),
+        cost_estimate=pl.CostEstimate(flops=2**26, bytes_accessed=2**21, transcendentals=0),
+    )(branch, residual, gain, w_first, extra)
     gained_all = lax.all_gather(gained, "zh", axis=0, tiled=True)
-    own_draws = samples // n_t * idx
-    extra = jnp.concatenate(
-        [
-            index_draws.reshape(rows, own_draws).astype(f32),
-            square_sum[:, None],
-            jnp.zeros((rows, 127 - own_draws), f32),
-        ],
-        axis=1,
-    )
-    first = jnp.concatenate([first, extra], axis=1).reshape(n_t, own, hidden + 128)
     first = exchange(first, TENSOR)
 
     pairs = own * samples
@@ -280,13 +314,12 @@
         out_shape=(
             jax.ShapeDtypeStruct((width, hidden), f32),
             jax.ShapeDtypeStruct((hidden_rows, reads), f32),
-            jax.ShapeDtypeStruct((8, 256), f32),
+            jax.ShapeDtypeStruct((hidden_cols, hidden_rows), f32),
         ),
         compiler_params=pltpu.CompilerParams(vmem_limit_bytes=24 * 2**20),
         cost_estimate=pl.CostEstimate(flops=0, bytes_accessed=4 * 2**20, transcendentals=0),
     )(grads)
-    grad_hidden = grad_hidden.reshape(8, 4, hidden_rows).transpose(2, 1, 0)
-    return (grad_first, grad_hidden.reshape(hidden_rows, hidden_cols), grad_output)
+    return (grad_first, grad_hidden.T, grad_output)
 
 
 def solution(mesh):

time: 217 us -> 216 us (level)
  no operation moved by 1% of the time
where the time goes in v4:
time: 216 us; the launch traced here: 213 us
  starting transfers between devices  76.5 us (35%)
  blocking collectives  63.9 us (30%)
  waiting for transfers between devices  50.2 us (23%)
  Pallas kernels  7.71 us (4%)
  local copies, waits for them, and re-layouts  6.82 us (3%)
  other arithmetic  4.82 us (2%)
    all_to_all x8, starting transfers between devices, exchange(): return lax.all_to_all(blocks, axes, 0, 0, tiled=True)  47.3 us
    all_to_all x8, waiting for transfers between devices, exchange(): return lax.all_to_all(blocks, axes, 0, 0, tiled=True)  40.5 us
    all_to_all x1, blocking collectives, exchange(): return lax.all_to_all(blocks, axes, 0, 0, tiled=True)  38.6 us
    ppermute x4, starting transfers between devices, from_further(): lax.ppermute(block, axis, [(i, (i - step) % count) for i in range(count)])  25.4 us
    all_gather x1, blocking collectives, shards(): gained_all = lax.all_gather(gained, 'zh', axis=0, tiled=True)  25.4 us
    ppermute x4, waiting for transfers between devices, from_further(): lax.ppermute(block, axis, [(i, (i - step) % count) for i in range(count)])  7.9 us
  transfers between devices with their start and end apart: 14, of which 10 were waited for; matrix products, arithmetic and copies ran while one was open for 3% of the time, Pallas kernels for 0%

profile of v4, /device:TPU:6, one launch (start us, length us, event | category | flops | bytes accessed | tf_op | source)
XLA Modules:
  0.0 213.1 jit_solution(1748902151754241925)
XLA Ops:
  0.7 1.7 broadcast_in_dim.52
  2.4 7.1 %all-to-all-start = ((bf16[8,64,512]{2,1,0:T(8,128)(2,1)}), bf16[8,64,512]{2,1,0:T(8,128)(2,1)S(1)}, u32[]{:S(2)}, u32[]{:S(2)}) async-start(bf16[8,64,512]{2,1,0:T(8,128)(2,1)} %broadcast_in_dim.52), calls=%async_computation | async-start | bytes 1048576 | tf_op jit(solution)/shard_map/all_to_all | solution.py:26
  9.5 6.1 %collective-permute-start.1 = (bf16[512,256]{1,0:T(8,128)(2,1)S(1)}, bf16[512,256]{1,0:T(8,128)(2,1)S(1)}, u32[]{:S(2)}, u32[]{:S(2)}) collective-permute-start(bf16[512,256]{1,0:T(8,128)(2,1)S(1)} %copy-done.6), channel_id=1, source_target_pairs={{0,128},{128,256},{256,384},{384,0},{1,129},{129,257},{257,385},{3... | collective-permute-start | bytes 786440 | tf_op jit(solution)/shard_map/ppermute | solution.py:35
  15.6 6.8 %collective-permute-start = (bf16[512,256]{1,0:T(8,128)(2,1)S(1)}, bf16[512,256]{1,0:T(8,128)(2,1)S(1)}, u32[]{:S(2)}, u32[]{:S(2)}) collective-permute-start(bf16[512,256]{1,0:T(8,128)(2,1)S(1)} %copy-done.6), channel_id=1, source_target_pairs={{0,384},{128,0},{256,128},{384,256},{1,385},{129,1},{257,129},{385... | collective-permute-start | bytes 786440 | tf_op jit(solution)/shard_map/ppermute | solution.py:35
  22.4 4.2 %collective-permute-done.1 = bf16[512,256]{1,0:T(8,128)(2,1)S(1)} collective-permute-done((bf16[512,256]{1,0:T(8,128)(2,1)S(1)}, bf16[512,256]{1,0:T(8,128)(2,1)S(1)}, u32[]{:S(2)}, u32[]{:S(2)}) %collective-permute-start.1) | collective-permute-done | bytes 262176 | tf_op jit(solution)/shard_map/ppermute | solution.py:35
  26.6 7.2 %collective-permute-start.3 = (bf16[256,256]{1,0:T(8,128)(2,1)S(1)}, bf16[256,256]{1,0:T(8,128)(2,1)S(1)}, u32[]{:S(2)}, u32[]{:S(2)}) collective-permute-start(bf16[256,256]{1,0:T(8,128)(2,1)S(1)} %slice.26), channel_id=1, source_target_pairs={{0,128},{128,256},{256,384},{384,0},{1,129},{129,257},{257,385},{3... | collective-permute-start | bytes 393224 | tf_op jit(solution)/shard_map/ppermute | solution.py:35
  33.8 5.4 %collective-permute-start.2 = (bf16[256,256]{1,0:T(8,128)(2,1)S(1)}, bf16[256,256]{1,0:T(8,128)(2,1)S(1)}, u32[]{:S(2)}, u32[]{:S(2)}) collective-permute-start(bf16[256,256]{1,0:T(8,128)(2,1)S(1)} %slice.24), channel_id=1, source_target_pairs={{0,384},{128,0},{256,128},{384,256},{1,385},{129,1},{257,129},{385... | collective-permute-start | bytes 393224 | tf_op jit(solution)/shard_map/ppermute | solution.py:35
  39.2 0.1 broadcast_in_dim.51
  39.3 0.4 fusion.4
  39.7 0.4 fusion.6
  40.0 0.4 fusion.8
  40.4 1.1 collective-permute-done.3
  41.5 0.3 fusion.10
  41.8 2.6 %collective-permute-done.2 = bf16[256,256]{1,0:T(8,128)(2,1)S(1)} collective-permute-done((bf16[256,256]{1,0:T(8,128)(2,1)S(1)}, bf16[256,256]{1,0:T(8,128)(2,1)S(1)}, u32[]{:S(2)}, u32[]{:S(2)}) %collective-permute-start.2) | collective-permute-done | bytes 131104 | tf_op jit(solution)/shard_map/ppermute | solution.py:35
  44.4 0.3 fusion.2
  44.7 1.9 collective-permute-start.4
  46.7 1.9 collective-permute-done.4
  48.5 0.9 fusion.9
  49.5 6.6 %all-to-all-start.1 = ((bf16[8,64,512]{2,1,0:T(8,128)(2,1)}), bf16[8,64,512]{2,1,0:T(8,128)(2,1)S(1)}, u32[]{:S(2)}, u32[]{:S(2)}) async-start(bf16[8,64,512]{2,1,0:T(8,128)(2,1)} %fusion.9), calls=%async_computation.1 | async-start | bytes 1048576 | tf_op jit(solution)/shard_map/all_to_all | solution.py:26
  56.0 0.1 copy.41
  56.1 0.1 copy.42
  56.3 0.1 reshape.164.residual_ref
  56.4 0.1 reshape.165
  56.5 0.1 copy.43
  56.6 0.3 broadcast_in_dim.57
  57.0 0.2 reshape.166.gain_ref
  57.2 0.1 copy.44
  57.2 0.4 copy-done.9
  57.6 0.1 copy.45
  57.7 0.4 copy-done.5
  58.2 0.2 copy.46
  58.4 0.1 pad.16.w_output_ref
  58.6 0.1 copy.51
  58.7 0.1 reshape.169
  58.9 5.1 %all-to-all-done.1.parts_ref = bf16[8,64,512]{2,1,0:T(8,128)(2,1)S(1)} async-done(((bf16[8,64,512]{2,1,0:T(8,128)(2,1)}), bf16[8,64,512]{2,1,0:T(8,128)(2,1)S(1)}, u32[]{:S(2)}, u32[]{:S(2)}) %all-to-all-start.1) | async-done | bytes 524320 | tf_op jit(solution)/shard_map/all_to_all | solution.py:26
  64.0 0.8 shard_map.139
  64.8 7.0 %all-to-all-start.2 = ((bf16[8,32,128]{2,1,0:T(8,128)(2,1)}), bf16[8,32,128]{2,1,0:T(8,128)(2,1)}, u32[]{:S(2)}, u32[]{:S(2)}) async-start(bf16[8,32,128]{2,1,0:T(8,128)(2,1)} %shard_map.139), calls=%async_computation.2 | async-start | bytes 131072 | tf_op jit(solution)/shard_map/all_to_all | solution.py:26
  71.8 8.5 %all-to-all-done.2 = bf16[8,32,128]{2,1,0:T(8,128)(2,1)} async-done(((bf16[8,32,128]{2,1,0:T(8,128)(2,1)}), bf16[8,32,128]{2,1,0:T(8,128)(2,1)}, u32[]{:S(2)}, u32[]{:S(2)}) %all-to-all-start.2) | async-done | bytes 65568 | tf_op jit(solution)/shard_map/all_to_all | solution.py:26
  80.3 3.3 %all-to-all-start.3 = ((bf16[4,64,128]{2,1,0:T(8,128)(2,1)}), bf16[4,64,128]{2,1,0:T(8,128)(2,1)S(1)}, u32[]{:S(2)}, u32[]{:S(2)}) async-start(bf16[4,64,128]{2,1,0:T(8,128)(2,1)} %bitcast.8), calls=%async_computation.3 | async-start | bytes 131072 | tf_op jit(solution)/shard_map/all_to_all | solution.py:26
  83.6 4.1 %all-to-all-done.3 = bf16[4,64,128]{2,1,0:T(8,128)(2,1)S(1)} async-done(((bf16[4,64,128]{2,1,0:T(8,128)(2,1)}), bf16[4,64,128]{2,1,0:T(8,128)(2,1)S(1)}, u32[]{:S(2)}, u32[]{:S(2)}) %all-to-all-start.3) | async-done | bytes 65568 | tf_op jit(solution)/shard_map/all_to_all | solution.py:26
  87.7 1.1 shard_map.140
  88.7 5.8 %all-to-all-start.4 = ((f32[16,4,1152]{2,1,0:T(4,128)}), f32[16,4,1152]{2,1,0:T(4,128)S(1)}, u32[]{:S(2)}, u32[]{:S(2)}) async-start(f32[16,4,1152]{2,1,0:T(4,128)} %get-tuple-element.16), calls=%async_computation.4 | async-start | bytes 589824 | tf_op jit(solution)/shard_map/all_to_all | solution.py:26
  94.5 0.1 compare_convert_fusion.same_ref
  94.6 6.0 %all-to-all-done.4.first_ref = f32[16,4,1152]{2,1,0:T(4,128)S(1)} async-done(((f32[16,4,1152]{2,1,0:T(4,128)}), f32[16,4,1152]{2,1,0:T(4,128)S(1)}, u32[]{:S(2)}, u32[]{:S(2)}) %all-to-all-start.4) | async-done | bytes 294944 | tf_op jit(solution)/shard_map/all_to_all | solution.py:26
  100.6 1.6 copy-done.1
  102.2 3.4 %shard_map.141 = (bf16[64,4,256]{2,1,0:T(4,128)(2,1)}, bf16[256,1024]{1,0:T(8,128)(2,1)S(1)}, bf16[256,1024]{1,0:T(8,128)(2,1)S(1)}, bf16[256,1024]{1,0:T(8,128)(2,1)S(1)}, bf16[256,256]{1,0:T(8,128)(2,1)S(1)}) custom-call(f32[16,4,1152]{2,1,0:T(4,128)S(1)} %all-to-all-done.4.first_ref, bf16[8,1280]{1,0:T(8,128)(2,1)S(1)} %pad_maximum_fusion.2.index_ref, ...), custom_call_target="tpu_custom_call" | custom-call | flops 2000000000 | bytes 8388608 | tf_op jit(solution)/shard_map/pallas_call | solution.py:259
  105.6 0.9 shard_map.142
  106.6 1.9 collective-permute-start.5
  108.5 9.0 %all-to-all-start.5 = ((bf16[64,4,256]{2,1,0:T(4,128)(2,1)}), bf16[64,4,256]{2,1,0:T(4,128)(2,1)S(1)}, u32[]{:S(2)}, u32[]{:S(2)}) async-start(bf16[64,4,256]{2,1,0:T(4,128)(2,1)} %get-tuple-element.17), calls=%async_computation.5 | async-start | bytes 262144 | tf_op jit(solution)/shard_map/all_to_all | solution.py:26
  117.5 2.7 %add_convert_fusion = bf16[8,64,1280]{2,1,0:T(8,128)(2,1)} fusion(bf16[8,64,1280]{2,1,0:T(8,128)(2,1)} %collective-permute-done.5, bf16[8,64,1280]{2,1,0:T(8,128)(2,1)S(1)} %get-tuple-element.22), kind=kLoop, calls=%fused_computation | loop fusion | flops 2621440 | bytes 3932160 | tf_op jit(solution)/shard_map/convert_element_type | solution.py:298
  120.2 6.6 %all-to-all-done.5 = bf16[64,4,256]{2,1,0:T(4,128)(2,1)S(1)} async-done(((bf16[64,4,256]{2,1,0:T(4,128)(2,1)}), bf16[64,4,256]{2,1,0:T(4,128)(2,1)S(1)}, u32[]{:S(2)}, u32[]{:S(2)}) %all-to-all-start.5) | async-done | bytes 131104 | tf_op jit(solution)/shard_map/all_to_all | solution.py:26
  126.8 5.1 %all-to-all-start.6 = ((bf16[8,64,1280]{2,1,0:T(8,128)(2,1)}), bf16[8,64,1280]{2,1,0:T(8,128)(2,1)S(1)}, u32[]{:S(2)}, u32[]{:S(2)}) async-start(bf16[8,64,1280]{2,1,0:T(8,128)(2,1)} %add_convert_fusion), calls=%async_computation.6 | async-start | bytes 2621440 | tf_op jit(solution)/shard_map/all_to_all | solution.py:26
  131.9 25.4 %all_gather.3 = bf16[256,512]{1,0:T(8,128)(2,1)S(1)} all-gather(bf16[64,512]{1,0:T(8,128)(2,1)S(1)} %get-tuple-element.15), channel_id=1, replica_groups=mesh['zh'=4,'y'=8,'x'=4,'zl'=2,'c'=2] {'zh'}, dimensions={0}, use_global_device_ids=true | all-gather | bytes 327680 | tf_op jit(solution)/shard_map/all_gather | solution.py:254
  157.4 0.3 convolution_convert_fusion
  157.7 0.2 reduce_sum.24
  157.9 0.7 pad_maximum_fusion.1
  158.6 3.4 %all-to-all-start.7 = ((bf16[8,72,256]{2,1,0:T(8,128)(2,1)}), bf16[8,72,256]{2,1,0:T(8,128)(2,1)S(1)}, u32[]{:S(2)}, u32[]{:S(2)}) async-start(bf16[8,72,256]{2,1,0:T(8,128)(2,1)} %pad_maximum_fusion.1), calls=%async_computation.7 | async-start | bytes 589824 | tf_op jit(solution)/shard_map/all_to_all | solution.py:26
  162.0 0.2 copy.48
  162.2 0.1 copy.49
  162.3 0.2 reshape.175
  162.5 10.2 %all-to-all-done.7 = bf16[8,72,256]{2,1,0:T(8,128)(2,1)S(1)} async-done(((bf16[8,72,256]{2,1,0:T(8,128)(2,1)}), bf16[8,72,256]{2,1,0:T(8,128)(2,1)S(1)}, u32[]{:S(2)}, u32[]{:S(2)}) %all-to-all-start.7) | async-done | bytes 294944 | tf_op jit(solution)/shard_map/all_to_all | solution.py:26
  172.9 0.1 pad_maximum_fusion
  173.0 38.6 %all_to_all.45.blocks_ref = bf16[32,80,256]{2,1,0:T(8,128)(2,1)S(1)} all-to-all(bf16[32,80,256]{2,1,0:T(8,128)(2,1)S(1)} %pad_maximum_fusion), channel_id=1, replica_groups=mesh['zh'=4,'y'=8,'x'=4,'zl'=2,'c'=2] {'zh','y'}, dimensions={0} | all-to-all | bytes 2621440 | tf_op jit(solution)/shard_map/all_to_all | solution.py:26
  211.6 1.5 shard_map.143
  (41 shorter events, 0.5 us)
Async XLA Ops:
  0.6 57.8 %copy-start = (s32[64,25]{0,1:T(8,128)S(1)}, s32[64,25]{0,1:T(8,128)}, u32[]{:S(2)}) copy-start(s32[64,25]{0,1:T(8,128)} %param.17) | copy-start | bytes 19204
  0.6 8.8 %copy-start.6 = (bf16[512,256]{1,0:T(8,128)(2,1)S(1)}, bf16[512,256]{1,0:T(8,128)(2,1)}, u32[]{:S(2)}) copy-start(bf16[512,256]{1,0:T(8,128)(2,1)} %param.14) | copy-start | bytes 786436
  2.4 36.8 %all-to-all-start = ((bf16[8,64,512]{2,1,0:T(8,128)(2,1)}), bf16[8,64,512]{2,1,0:T(8,128)(2,1)S(1)}, u32[]{:S(2)}, u32[]{:S(2)}) async-start(bf16[8,64,512]{2,1,0:T(8,128)(2,1)} %broadcast_in_dim.52), calls=%async_computation | async-start | bytes 1048576 | tf_op jit(solution)/shard_map/all_to_all | solution.py:26
  9.5 17.1 %collective-permute-start.1 = (bf16[512,256]{1,0:T(8,128)(2,1)S(1)}, bf16[512,256]{1,0:T(8,128)(2,1)S(1)}, u32[]{:S(2)}, u32[]{:S(2)}) collective-permute-start(bf16[512,256]{1,0:T(8,128)(2,1)S(1)} %copy-done.6), channel_id=1, source_target_pairs={{0,128},{128,256},{256,384},{384,0},{1,129},{129,257},{257,385},{3... | collective-permute-start | bytes 786440 | tf_op jit(solution)/shard_map/ppermute | solution.py:35
  15.6 18.2 %collective-permute-start = (bf16[512,256]{1,0:T(8,128)(2,1)S(1)}, bf16[512,256]{1,0:T(8,128)(2,1)S(1)}, u32[]{:S(2)}, u32[]{:S(2)}) collective-permute-start(bf16[512,256]{1,0:T(8,128)(2,1)S(1)} %copy-done.6), channel_id=1, source_target_pairs={{0,384},{128,0},{256,128},{384,256},{1,385},{129,1},{257,129},{385... | collective-permute-start | bytes 786440 | tf_op jit(solution)/shard_map/ppermute | solution.py:35
  26.6 14.9 %collective-permute-start.3 = (bf16[256,256]{1,0:T(8,128)(2,1)S(1)}, bf16[256,256]{1,0:T(8,128)(2,1)S(1)}, u32[]{:S(2)}, u32[]{:S(2)}) collective-permute-start(bf16[256,256]{1,0:T(8,128)(2,1)S(1)} %slice.26), channel_id=1, source_target_pairs={{0,128},{128,256},{256,384},{384,0},{1,129},{129,257},{257,385},{3... | collective-permute-start | bytes 393224 | tf_op jit(solution)/shard_map/ppermute | solution.py:35
  33.8 10.6 %collective-permute-start.2 = (bf16[256,256]{1,0:T(8,128)(2,1)S(1)}, bf16[256,256]{1,0:T(8,128)(2,1)S(1)}, u32[]{:S(2)}, u32[]{:S(2)}) collective-permute-start(bf16[256,256]{1,0:T(8,128)(2,1)S(1)} %slice.24), channel_id=1, source_target_pairs={{0,384},{128,0},{256,128},{384,256},{1,385},{129,1},{257,129},{385... | collective-permute-start | bytes 393224 | tf_op jit(solution)/shard_map/ppermute | solution.py:35
  44.7 3.8 %collective-permute-start.4 = (bf16[8,64,512]{2,1,0:T(8,128)(2,1)S(1)}, bf16[8,64,512]{2,1,0:T(8,128)(2,1)S(1)}, u32[]{:S(2)}, u32[]{:S(2)}) collective-permute-start(bf16[8,64,512]{2,1,0:T(8,128)(2,1)S(1)} %dynamic-slice_bitcast_fusion), channel_id=1, source_target_pairs={{0,1},{1,0},{2,3},{3,2},{4,5},{5,4},{6,7},{7,6},{8,9},{9,8},{10,11... | collective-permute-start | bytes 1572872 | tf_op jit(solution)/shard_map/ppermute | solution.py:227
  46.6 9.4 %copy-start.7 = (bf16[64,512]{1,0:T(8,128)(2,1)S(1)}, bf16[64,512]{1,0:T(8,128)(2,1)}, u32[]{:S(2)}) copy-start(bf16[64,512]{1,0:T(8,128)(2,1)} %param.12) | copy-start | bytes 196612
  46.7 9.7 %copy-start.10 = (f32[512]{0:T(512)S(1)}, f32[512]{0:T(512)}, u32[]{:S(2)}) copy-start(f32[512]{0:T(512)} %param.15) | copy-start | bytes 6148
  49.5 7.7 %copy-start.4 = (bf16[512,1024]{1,0:T(8,128)(2,1)S(1)}, bf16[512,1024]{1,0:T(8,128)(2,1)}, u32[]{:S(2)}) copy-start(bf16[512,1024]{1,0:T(8,128)(2,1)} %param.18) | copy-start | bytes 3145732
  49.5 14.6 %all-to-all-start.1 = ((bf16[8,64,512]{2,1,0:T(8,128)(2,1)}), bf16[8,64,512]{2,1,0:T(8,128)(2,1)S(1)}, u32[]{:S(2)}, u32[]{:S(2)}) async-start(bf16[8,64,512]{2,1,0:T(8,128)(2,1)} %fusion.9), calls=%async_computation.1 | async-start | bytes 1048576 | tf_op jit(solution)/shard_map/all_to_all | solution.py:26
  56.9 0.7 copy-start.9
  57.1 1.0 copy-start.5
  58.9 35.7 %copy-start.8 = (bf16[8,1024]{1,0:T(8,128)(2,1)S(1)}, bf16[8,1024]{1,0:T(8,128)(2,1)}, u32[]{:S(2)}) copy-start(bf16[8,1024]{1,0:T(8,128)(2,1)} %param.19) | copy-start | bytes 49156
  64.8 35.8 %copy-start.2 = (f32[1024]{0:T(1024)S(1)}, f32[1024]{0:T(1024)}, u32[]{:S(2)}) copy-start(f32[1024]{0:T(1024)} %param.20) | copy-start | bytes 12292
  64.8 35.8 %copy-start.3 = (f32[1024]{0:T(1024)S(1)}, f32[1024]{0:T(1024)}, u32[]{:S(2)}) copy-start(f32[1024]{0:T(1024)} %param.22) | copy-start | bytes 12292
  64.8 15.5 %all-to-all-start.2 = ((bf16[8,32,128]{2,1,0:T(8,128)(2,1)}), bf16[8,32,128]{2,1,0:T(8,128)(2,1)}, u32[]{:S(2)}, u32[]{:S(2)}) async-start(bf16[8,32,128]{2,1,0:T(8,128)(2,1)} %shard_map.139), calls=%async_computation.2 | async-start | bytes 131072 | tf_op jit(solution)/shard_map/all_to_all | solution.py:26
  80.3 7.4 %all-to-all-start.3 = ((bf16[4,64,128]{2,1,0:T(8,128)(2,1)}), bf16[4,64,128]{2,1,0:T(8,128)(2,1)S(1)}, u32[]{:S(2)}, u32[]{:S(2)}) async-start(bf16[4,64,128]{2,1,0:T(8,128)(2,1)} %bitcast.8), calls=%async_computation.3 | async-start | bytes 131072 | tf_op jit(solution)/shard_map/all_to_all | solution.py:26
  88.7 11.9 %all-to-all-start.4 = ((f32[16,4,1152]{2,1,0:T(4,128)}), f32[16,4,1152]{2,1,0:T(4,128)S(1)}, u32[]{:S(2)}, u32[]{:S(2)}) async-start(f32[16,4,1152]{2,1,0:T(4,128)} %get-tuple-element.16), calls=%async_computation.4 | async-start | bytes 589824 | tf_op jit(solution)/shard_map/all_to_all | solution.py:26
  100.6 1.6 copy-start.1
  106.6 11.0 %collective-permute-start.5 = (bf16[8,64,1280]{2,1,0:T(8,128)(2,1)S(1)}, bf16[8,64,1280]{2,1,0:T(8,128)(2,1)}, u32[]{:S(2)}, u32[]{:S(2)}) collective-permute-start(bf16[8,64,1280]{2,1,0:T(8,128)(2,1)S(1)} %get-tuple-element.23), channel_id=1, source_target_pairs={{0,1},{1,0},{2,3},{3,2},{4,5},{5,4},{6,7},{7,6},{8,9},{9,8},{10,11... | collective-permute-start | bytes 3932168 | tf_op jit(solution)/shard_map/ppermute | solution.py:297
  108.5 18.3 %all-to-all-start.5 = ((bf16[64,4,256]{2,1,0:T(4,128)(2,1)}), bf16[64,4,256]{2,1,0:T(4,128)(2,1)S(1)}, u32[]{:S(2)}, u32[]{:S(2)}) async-start(bf16[64,4,256]{2,1,0:T(4,128)(2,1)} %get-tuple-element.17), calls=%async_computation.5 | async-start | bytes 262144 | tf_op jit(solution)/shard_map/all_to_all | solution.py:26
  126.8 30.8 %all-to-all-start.6 = ((bf16[8,64,1280]{2,1,0:T(8,128)(2,1)}), bf16[8,64,1280]{2,1,0:T(8,128)(2,1)S(1)}, u32[]{:S(2)}, u32[]{:S(2)}) async-start(bf16[8,64,1280]{2,1,0:T(8,128)(2,1)} %add_convert_fusion), calls=%async_computation.6 | async-start | bytes 2621440 | tf_op jit(solution)/shard_map/all_to_all | solution.py:26
  158.6 14.2 %all-to-all-start.7 = ((bf16[8,72,256]{2,1,0:T(8,128)(2,1)}), bf16[8,72,256]{2,1,0:T(8,128)(2,1)S(1)}, u32[]{:S(2)}, u32[]{:S(2)}) async-start(bf16[8,72,256]{2,1,0:T(8,128)(2,1)} %pad_maximum_fusion.1), calls=%async_computation.7 | async-start | bytes 589824 | tf_op jit(solution)/shard_map/all_to_all | solution.py:26

commit v5 on v4

--- a/solution.py
+++ b/solution.py
@@ -33,6 +33,11 @@
 def from_further(block, axis, step):
     count = PARTS[axis]
     return lax.ppermute(block, axis, [(i, (i - step) % count) for i in range(count)])
+
+
+def repeat_body(block_ref, blocks_ref):
+    for i in range(blocks_ref.shape[0]):
+        blocks_ref[i] = block_ref[...]
 
 
 def finish_body(blocks_ref, first_ref, output_ref, hidden_ref):
@@ -210,7 +215,13 @@
     own_labels = lax.dynamic_slice_in_dim(labels, tensor * own, own, 0).astype(f32)
     targets = jnp.broadcast_to(own_labels[:, :, None], (own, classes, idx)).reshape(own, reads)
     targets = jnp.pad(targets, ((0, 0), (0, 256 - reads)))
-    att = spread(attention, "y", n_y).reshape(n_y * rows, width)
+    att = pl.pallas_call(
+        repeat_body,
+        out_shape=jax.ShapeDtypeStruct((n_y, rows, width), bf16),
+        compiler_params=pltpu.CompilerParams(vmem_limit_bytes=16 * 2**20),
+        cost_estimate=pl.CostEstimate(flops=0, bytes_accessed=9 * 2**16, transcendentals=0),
+    )(attention)
+    att = exchange(att, "y").reshape(n_y * rows, width)
     half = width // 2
     ahead, behind = from_further(out_proj, "zh", 1), from_further(out_proj, "zh", -1)
     opposite = [from_further(ahead[:half], "zh", 1), from_further(behind[half:], "zh", -1)]

time: 216 us -> 216 us (level)
  no operation moved by 1% of the time
where the time goes in v5:
time: 216 us; the launch traced here: 213 us
  starting transfers between devices  76.5 us (35%)
  blocking collectives  63.9 us (30%)
  waiting for transfers between devices  50.2 us (23%)
  Pallas kernels  8.55 us (4%)
  local copies, waits for them, and re-layouts  5.94 us (3%)
  other arithmetic  4.82 us (2%)
    all_to_all x8, starting transfers between devices, exchange(): return lax.all_to_all(blocks, axes, 0, 0, tiled=True)  47.3 us
    all_to_all x8, waiting for transfers between devices, exchange(): return lax.all_to_all(blocks, axes, 0, 0, tiled=True)  40.5 us
    all_to_all x1, blocking collectives, exchange(): return lax.all_to_all(blocks, axes, 0, 0, tiled=True)  38.6 us
    ppermute x4, starting transfers between devices, from_further(): lax.ppermute(block, axis, [(i, (i - step) % count) for i in range(count)])  25.4 us
    all_gather x1, blocking collectives, shards(): gained_all = lax.all_gather(gained, 'zh', axis=0, tiled=True)  25.4 us
    ppermute x4, waiting for transfers between devices, from_further(): lax.ppermute(block, axis, [(i, (i - step) % count) for i in range(count)])  7.9 us
  transfers between devices with their start and end apart: 14, of which 10 were waited for; matrix products, arithmetic and copies ran while one was open for 3% of the time, Pallas kernels for 0%

profile of v5, /device:TPU:6, one launch (start us, length us, event | category | flops | bytes accessed | tf_op | source)
XLA Modules:
  0.0 213.0 jit_solution(9354318498186723250)
XLA Ops:
  0.7 0.8 copy-done.1
  1.5 0.8 shard_map.139
  2.3 7.1 %all-to-all-start = ((bf16[8,64,512]{2,1,0:T(8,128)(2,1)}), bf16[8,64,512]{2,1,0:T(8,128)(2,1)S(1)}, u32[]{:S(2)}, u32[]{:S(2)}) async-start(bf16[8,64,512]{2,1,0:T(8,128)(2,1)} %shard_map.139), calls=%async_computation | async-start | bytes 1048576 | tf_op jit(solution)/shard_map/all_to_all | solution.py:26
  9.4 6.1 %collective-permute-start.1 = (bf16[512,256]{1,0:T(8,128)(2,1)S(1)}, bf16[512,256]{1,0:T(8,128)(2,1)S(1)}, u32[]{:S(2)}, u32[]{:S(2)}) collective-permute-start(bf16[512,256]{1,0:T(8,128)(2,1)S(1)} %copy-done.7), channel_id=1, source_target_pairs={{0,128},{128,256},{256,384},{384,0},{1,129},{129,257},{257,385},{3... | collective-permute-start | bytes 786440 | tf_op jit(solution)/shard_map/ppermute | solution.py:35
  15.5 6.8 %collective-permute-start = (bf16[512,256]{1,0:T(8,128)(2,1)S(1)}, bf16[512,256]{1,0:T(8,128)(2,1)S(1)}, u32[]{:S(2)}, u32[]{:S(2)}) collective-permute-start(bf16[512,256]{1,0:T(8,128)(2,1)S(1)} %copy-done.7), channel_id=1, source_target_pairs={{0,384},{128,0},{256,128},{384,256},{1,385},{129,1},{257,129},{385... | collective-permute-start | bytes 786440 | tf_op jit(solution)/shard_map/ppermute | solution.py:35
  22.4 4.2 %collective-permute-done.1 = bf16[512,256]{1,0:T(8,128)(2,1)S(1)} collective-permute-done((bf16[512,256]{1,0:T(8,128)(2,1)S(1)}, bf16[512,256]{1,0:T(8,128)(2,1)S(1)}, u32[]{:S(2)}, u32[]{:S(2)}) %collective-permute-start.1) | collective-permute-done | bytes 262176 | tf_op jit(solution)/shard_map/ppermute | solution.py:35
  26.5 7.2 %collective-permute-start.3 = (bf16[256,256]{1,0:T(8,128)(2,1)S(1)}, bf16[256,256]{1,0:T(8,128)(2,1)S(1)}, u32[]{:S(2)}, u32[]{:S(2)}) collective-permute-start(bf16[256,256]{1,0:T(8,128)(2,1)S(1)} %slice.26), channel_id=1, source_target_pairs={{0,128},{128,256},{256,384},{384,0},{1,129},{129,257},{257,385},{3... | collective-permute-start | bytes 393224 | tf_op jit(solution)/shard_map/ppermute | solution.py:35
  33.7 5.4 %collective-permute-start.2 = (bf16[256,256]{1,0:T(8,128)(2,1)S(1)}, bf16[256,256]{1,0:T(8,128)(2,1)S(1)}, u32[]{:S(2)}, u32[]{:S(2)}) collective-permute-start(bf16[256,256]{1,0:T(8,128)(2,1)S(1)} %slice.24), channel_id=1, source_target_pairs={{0,384},{128,0},{256,128},{384,256},{1,385},{129,1},{257,129},{385... | collective-permute-start | bytes 393224 | tf_op jit(solution)/shard_map/ppermute | solution.py:35
  39.3 0.4 fusion.4
  39.6 0.4 fusion.6
  40.0 0.4 fusion.8
  40.3 1.1 collective-permute-done.3
  41.4 0.3 fusion.10
  41.7 2.6 %collective-permute-done.2 = bf16[256,256]{1,0:T(8,128)(2,1)S(1)} collective-permute-done((bf16[256,256]{1,0:T(8,128)(2,1)S(1)}, bf16[256,256]{1,0:T(8,128)(2,1)S(1)}, u32[]{:S(2)}, u32[]{:S(2)}) %collective-permute-start.2) | collective-permute-done | bytes 131104 | tf_op jit(solution)/shard_map/ppermute | solution.py:35
  44.3 0.3 fusion.2
  44.7 1.9 collective-permute-start.4
  46.6 1.9 collective-permute-done.4
  48.5 0.9 fusion.9
  49.4 6.6 %all-to-all-start.1 = ((bf16[8,64,512]{2,1,0:T(8,128)(2,1)}), bf16[8,64,512]{2,1,0:T(8,128)(2,1)S(1)}, u32[]{:S(2)}, u32[]{:S(2)}) async-start(bf16[8,64,512]{2,1,0:T(8,128)(2,1)} %fusion.9), calls=%async_computation.1 | async-start | bytes 1048576 | tf_op jit(solution)/shard_map/all_to_all | solution.py:26
  56.0 0.1 copy.41
  56.1 0.1 copy.42
  56.2 0.1 reshape.163.residual_ref
  56.3 0.1 reshape.164
  56.4 0.1 copy.43
  56.6 0.3 broadcast_in_dim.50
  56.9 0.2 reshape.165.gain_ref
  57.1 0.1 copy.44
  57.2 0.4 copy-done.10
  57.6 0.1 copy.45
  57.7 0.4 copy-done.6
  58.1 0.2 copy.46
  58.3 0.1 pad.16.w_output_ref
  58.5 0.1 copy.51
  58.7 0.1 reshape.168
  58.8 5.1 %all-to-all-done.1.parts_ref = bf16[8,64,512]{2,1,0:T(8,128)(2,1)S(1)} async-done(((bf16[8,64,512]{2,1,0:T(8,128)(2,1)}), bf16[8,64,512]{2,1,0:T(8,128)(2,1)S(1)}, u32[]{:S(2)}, u32[]{:S(2)}) %all-to-all-start.1) | async-done | bytes 524320 | tf_op jit(solution)/shard_map/all_to_all | solution.py:26
  64.0 0.8 shard_map.140
  64.8 7.0 %all-to-all-start.2 = ((bf16[8,32,128]{2,1,0:T(8,128)(2,1)}), bf16[8,32,128]{2,1,0:T(8,128)(2,1)}, u32[]{:S(2)}, u32[]{:S(2)}) async-start(bf16[8,32,128]{2,1,0:T(8,128)(2,1)} %shard_map.140), calls=%async_computation.2 | async-start | bytes 131072 | tf_op jit(solution)/shard_map/all_to_all | solution.py:26
  71.8 8.5 %all-to-all-done.2 = bf16[8,32,128]{2,1,0:T(8,128)(2,1)} async-done(((bf16[8,32,128]{2,1,0:T(8,128)(2,1)}), bf16[8,32,128]{2,1,0:T(8,128)(2,1)}, u32[]{:S(2)}, u32[]{:S(2)}) %all-to-all-start.2) | async-done | bytes 65568 | tf_op jit(solution)/shard_map/all_to_all | solution.py:26
  80.2 3.3 %all-to-all-start.3 = ((bf16[4,64,128]{2,1,0:T(8,128)(2,1)}), bf16[4,64,128]{2,1,0:T(8,128)(2,1)S(1)}, u32[]{:S(2)}, u32[]{:S(2)}) async-start(bf16[4,64,128]{2,1,0:T(8,128)(2,1)} %bitcast.8), calls=%async_computation.3 | async-start | bytes 131072 | tf_op jit(solution)/shard_map/all_to_all | solution.py:26
  83.5 4.1 %all-to-all-done.3 = bf16[4,64,128]{2,1,0:T(8,128)(2,1)S(1)} async-done(((bf16[4,64,128]{2,1,0:T(8,128)(2,1)}), bf16[4,64,128]{2,1,0:T(8,128)(2,1)S(1)}, u32[]{:S(2)}, u32[]{:S(2)}) %all-to-all-start.3) | async-done | bytes 65568 | tf_op jit(solution)/shard_map/all_to_all | solution.py:26
  87.6 1.1 shard_map.141
  88.7 5.8 %all-to-all-start.4 = ((f32[16,4,1152]{2,1,0:T(4,128)}), f32[16,4,1152]{2,1,0:T(4,128)S(1)}, u32[]{:S(2)}, u32[]{:S(2)}) async-start(f32[16,4,1152]{2,1,0:T(4,128)} %get-tuple-element.16), calls=%async_computation.4 | async-start | bytes 589824 | tf_op jit(solution)/shard_map/all_to_all | solution.py:26
  94.5 0.1 compare_convert_fusion.same_ref
  94.6 6.0 %all-to-all-done.4.first_ref = f32[16,4,1152]{2,1,0:T(4,128)S(1)} async-done(((f32[16,4,1152]{2,1,0:T(4,128)}), f32[16,4,1152]{2,1,0:T(4,128)S(1)}, u32[]{:S(2)}, u32[]{:S(2)}) %all-to-all-start.4) | async-done | bytes 294944 | tf_op jit(solution)/shard_map/all_to_all | solution.py:26
  100.6 1.6 copy-done.2
  102.2 3.4 %shard_map.142 = (bf16[64,4,256]{2,1,0:T(4,128)(2,1)}, bf16[256,1024]{1,0:T(8,128)(2,1)S(1)}, bf16[256,1024]{1,0:T(8,128)(2,1)S(1)}, bf16[256,1024]{1,0:T(8,128)(2,1)S(1)}, bf16[256,256]{1,0:T(8,128)(2,1)S(1)}) custom-call(f32[16,4,1152]{2,1,0:T(4,128)S(1)} %all-to-all-done.4.first_ref, bf16[8,1280]{1,0:T(8,128)(2,1)S(1)} %pad_maximum_fusion.2.index_ref, ...), custom_call_target="tpu_custom_call" | custom-call | flops 2000000000 | bytes 8388608 | tf_op jit(solution)/shard_map/pallas_call | solution.py:270
  105.6 1.0 shard_map.143
  106.5 1.9 collective-permute-start.5
  108.5 9.0 %all-to-all-start.5 = ((bf16[64,4,256]{2,1,0:T(4,128)(2,1)}), bf16[64,4,256]{2,1,0:T(4,128)(2,1)S(1)}, u32[]{:S(2)}, u32[]{:S(2)}) async-start(bf16[64,4,256]{2,1,0:T(4,128)(2,1)} %get-tuple-element.17), calls=%async_computation.5 | async-start | bytes 262144 | tf_op jit(solution)/shard_map/all_to_all | solution.py:26
  117.5 2.7 %add_convert_fusion = bf16[8,64,1280]{2,1,0:T(8,128)(2,1)} fusion(bf16[8,64,1280]{2,1,0:T(8,128)(2,1)} %collective-permute-done.5, bf16[8,64,1280]{2,1,0:T(8,128)(2,1)S(1)} %get-tuple-element.22), kind=kLoop, calls=%fused_computation | loop fusion | flops 2621440 | bytes 3932160 | tf_op jit(solution)/shard_map/convert_element_type | solution.py:309
  120.2 6.6 %all-to-all-done.5 = bf16[64,4,256]{2,1,0:T(4,128)(2,1)S(1)} async-done(((bf16[64,4,256]{2,1,0:T(4,128)(2,1)}), bf16[64,4,256]{2,1,0:T(4,128)(2,1)S(1)}, u32[]{:S(2)}, u32[]{:S(2)}) %all-to-all-start.5) | async-done | bytes 131104 | tf_op jit(solution)/shard_map/all_to_all | solution.py:26
  126.8 5.1 %all-to-all-start.6 = ((bf16[8,64,1280]{2,1,0:T(8,128)(2,1)}), bf16[8,64,1280]{2,1,0:T(8,128)(2,1)S(1)}, u32[]{:S(2)}, u32[]{:S(2)}) async-start(bf16[8,64,1280]{2,1,0:T(8,128)(2,1)} %add_convert_fusion), calls=%async_computation.6 | async-start | bytes 2621440 | tf_op jit(solution)/shard_map/all_to_all | solution.py:26
  131.9 25.4 %all_gather.3 = bf16[256,512]{1,0:T(8,128)(2,1)S(1)} all-gather(bf16[64,512]{1,0:T(8,128)(2,1)S(1)} %get-tuple-element.15), channel_id=1, replica_groups=mesh['zh'=4,'y'=8,'x'=4,'zl'=2,'c'=2] {'zh'}, dimensions={0}, use_global_device_ids=true | all-gather | bytes 327680 | tf_op jit(solution)/shard_map/all_gather | solution.py:265
  157.3 0.3 convolution_convert_fusion
  157.6 0.2 reduce_sum.24
  157.8 0.7 pad_maximum_fusion.1
  158.6 3.4 %all-to-all-start.7 = ((bf16[8,72,256]{2,1,0:T(8,128)(2,1)}), bf16[8,72,256]{2,1,0:T(8,128)(2,1)S(1)}, u32[]{:S(2)}, u32[]{:S(2)}) async-start(bf16[8,72,256]{2,1,0:T(8,128)(2,1)} %pad_maximum_fusion.1), calls=%async_computation.7 | async-start | bytes 589824 | tf_op jit(solution)/shard_map/all_to_all | solution.py:26
  162.0 0.2 copy.48
  162.2 0.1 copy.49
  162.3 0.2 reshape.174
  162.5 10.2 %all-to-all-done.7 = bf16[8,72,256]{2,1,0:T(8,128)(2,1)S(1)} async-done(((bf16[8,72,256]{2,1,0:T(8,128)(2,1)}), bf16[8,72,256]{2,1,0:T(8,128)(2,1)S(1)}, u32[]{:S(2)}, u32[]{:S(2)}) %all-to-all-start.7) | async-done | bytes 294944 | tf_op jit(solution)/shard_map/all_to_all | solution.py:26
  172.9 0.1 pad_maximum_fusion
  173.0 38.6 %all_to_all.45.blocks_ref = bf16[32,80,256]{2,1,0:T(8,128)(2,1)S(1)} all-to-all(bf16[32,80,256]{2,1,0:T(8,128)(2,1)S(1)} %pad_maximum_fusion), channel_id=1, replica_groups=mesh['zh'=4,'y'=8,'x'=4,'zl'=2,'c'=2] {'zh','y'}, dimensions={0} | all-to-all | bytes 2621440 | tf_op jit(solution)/shard_map/all_to_all | solution.py:26
  211.5 1.5 shard_map.144
  (43 shorter events, 0.6 us)
Async XLA Ops:
  0.6 57.8 %copy-start = (s32[64,25]{0,1:T(8,128)S(1)}, s32[64,25]{0,1:T(8,128)}, u32[]{:S(2)}) copy-start(s32[64,25]{0,1:T(8,128)} %param.17) | copy-start | bytes 19204
  0.6 0.8 copy-start.1
  1.5 7.9 %copy-start.7 = (bf16[512,256]{1,0:T(8,128)(2,1)S(1)}, bf16[512,256]{1,0:T(8,128)(2,1)}, u32[]{:S(2)}) copy-start(bf16[512,256]{1,0:T(8,128)(2,1)} %param.14) | copy-start | bytes 786436
  2.3 36.8 %all-to-all-start = ((bf16[8,64,512]{2,1,0:T(8,128)(2,1)}), bf16[8,64,512]{2,1,0:T(8,128)(2,1)S(1)}, u32[]{:S(2)}, u32[]{:S(2)}) async-start(bf16[8,64,512]{2,1,0:T(8,128)(2,1)} %shard_map.139), calls=%async_computation | async-start | bytes 1048576 | tf_op jit(solution)/shard_map/all_to_all | solution.py:26
  9.4 17.1 %collective-permute-start.1 = (bf16[512,256]{1,0:T(8,128)(2,1)S(1)}, bf16[512,256]{1,0:T(8,128)(2,1)S(1)}, u32[]{:S(2)}, u32[]{:S(2)}) collective-permute-start(bf16[512,256]{1,0:T(8,128)(2,1)S(1)} %copy-done.7), channel_id=1, source_target_pairs={{0,128},{128,256},{256,384},{384,0},{1,129},{129,257},{257,385},{3... | collective-permute-start | bytes 786440 | tf_op jit(solution)/shard_map/ppermute | solution.py:35
  15.5 18.2 %collective-permute-start = (bf16[512,256]{1,0:T(8,128)(2,1)S(1)}, bf16[512,256]{1,0:T(8,128)(2,1)S(1)}, u32[]{:S(2)}, u32[]{:S(2)}) collective-permute-start(bf16[512,256]{1,0:T(8,128)(2,1)S(1)} %copy-done.7), channel_id=1, source_target_pairs={{0,384},{128,0},{256,128},{384,256},{1,385},{129,1},{257,129},{385... | collective-permute-start | bytes 786440 | tf_op jit(solution)/shard_map/ppermute | solution.py:35
  26.5 14.9 %collective-permute-start.3 = (bf16[256,256]{1,0:T(8,128)(2,1)S(1)}, bf16[256,256]{1,0:T(8,128)(2,1)S(1)}, u32[]{:S(2)}, u32[]{:S(2)}) collective-permute-start(bf16[256,256]{1,0:T(8,128)(2,1)S(1)} %slice.26), channel_id=1, source_target_pairs={{0,128},{128,256},{256,384},{384,0},{1,129},{129,257},{257,385},{3... | collective-permute-start | bytes 393224 | tf_op jit(solution)/shard_map/ppermute | solution.py:35
  33.7 10.6 %collective-permute-start.2 = (bf16[256,256]{1,0:T(8,128)(2,1)S(1)}, bf16[256,256]{1,0:T(8,128)(2,1)S(1)}, u32[]{:S(2)}, u32[]{:S(2)}) collective-permute-start(bf16[256,256]{1,0:T(8,128)(2,1)S(1)} %slice.24), channel_id=1, source_target_pairs={{0,384},{128,0},{256,128},{384,256},{1,385},{129,1},{257,129},{385... | collective-permute-start | bytes 393224 | tf_op jit(solution)/shard_map/ppermute | solution.py:35
  44.7 3.8 %collective-permute-start.4 = (bf16[8,64,512]{2,1,0:T(8,128)(2,1)S(1)}, bf16[8,64,512]{2,1,0:T(8,128)(2,1)S(1)}, u32[]{:S(2)}, u32[]{:S(2)}) collective-permute-start(bf16[8,64,512]{2,1,0:T(8,128)(2,1)S(1)} %dynamic-slice_bitcast_fusion), channel_id=1, source_target_pairs={{0,1},{1,0},{2,3},{3,2},{4,5},{5,4},{6,7},{7,6},{8,9},{9,8},{10,11... | collective-permute-start | bytes 1572872 | tf_op jit(solution)/shard_map/ppermute | solution.py:238
  46.6 9.4 %copy-start.8 = (bf16[64,512]{1,0:T(8,128)(2,1)S(1)}, bf16[64,512]{1,0:T(8,128)(2,1)}, u32[]{:S(2)}) copy-start(bf16[64,512]{1,0:T(8,128)(2,1)} %param.12) | copy-start | bytes 196612
  46.6 9.7 %copy-start.11 = (f32[512]{0:T(512)S(1)}, f32[512]{0:T(512)}, u32[]{:S(2)}) copy-start(f32[512]{0:T(512)} %param.15) | copy-start | bytes 6148
  49.4 7.7 %copy-start.5 = (bf16[512,1024]{1,0:T(8,128)(2,1)S(1)}, bf16[512,1024]{1,0:T(8,128)(2,1)}, u32[]{:S(2)}) copy-start(bf16[512,1024]{1,0:T(8,128)(2,1)} %param.18) | copy-start | bytes 3145732
  49.4 14.6 %all-to-all-start.1 = ((bf16[8,64,512]{2,1,0:T(8,128)(2,1)}), bf16[8,64,512]{2,1,0:T(8,128)(2,1)S(1)}, u32[]{:S(2)}, u32[]{:S(2)}) async-start(bf16[8,64,512]{2,1,0:T(8,128)(2,1)} %fusion.9), calls=%async_computation.1 | async-start | bytes 1048576 | tf_op jit(solution)/shard_map/all_to_all | solution.py:26
  56.9 0.7 copy-start.10
  57.1 1.0 copy-start.6
  58.8 35.6 %copy-start.9 = (bf16[8,1024]{1,0:T(8,128)(2,1)S(1)}, bf16[8,1024]{1,0:T(8,128)(2,1)}, u32[]{:S(2)}) copy-start(bf16[8,1024]{1,0:T(8,128)(2,1)} %param.19) | copy-start | bytes 49156
  64.8 35.8 %copy-start.3 = (f32[1024]{0:T(1024)S(1)}, f32[1024]{0:T(1024)}, u32[]{:S(2)}) copy-start(f32[1024]{0:T(1024)} %param.20) | copy-start | bytes 12292
  64.8 35.8 %copy-start.4 = (f32[1024]{0:T(1024)S(1)}, f32[1024]{0:T(1024)}, u32[]{:S(2)}) copy-start(f32[1024]{0:T(1024)} %param.22) | copy-start | bytes 12292
  64.8 15.5 %all-to-all-start.2 = ((bf16[8,32,128]{2,1,0:T(8,128)(2,1)}), bf16[8,32,128]{2,1,0:T(8,128)(2,1)}, u32[]{:S(2)}, u32[]{:S(2)}) async-start(bf16[8,32,128]{2,1,0:T(8,128)(2,1)} %shard_map.140), calls=%async_computation.2 | async-start | bytes 131072 | tf_op jit(solution)/shard_map/all_to_all | solution.py:26
  80.2 7.4 %all-to-all-start.3 = ((bf16[4,64,128]{2,1,0:T(8,128)(2,1)}), bf16[4,64,128]{2,1,0:T(8,128)(2,1)S(1)}, u32[]{:S(2)}, u32[]{:S(2)}) async-start(bf16[4,64,128]{2,1,0:T(8,128)(2,1)} %bitcast.8), calls=%async_computation.3 | async-start | bytes 131072 | tf_op jit(solution)/shard_map/all_to_all | solution.py:26
  88.7 11.9 %all-to-all-start.4 = ((f32[16,4,1152]{2,1,0:T(4,128)}), f32[16,4,1152]{2,1,0:T(4,128)S(1)}, u32[]{:S(2)}, u32[]{:S(2)}) async-start(f32[16,4,1152]{2,1,0:T(4,128)} %get-tuple-element.16), calls=%async_computation.4 | async-start | bytes 589824 | tf_op jit(solution)/shard_map/all_to_all | solution.py:26
  100.6 1.6 copy-start.2
  106.5 11.0 %collective-permute-start.5 = (bf16[8,64,1280]{2,1,0:T(8,128)(2,1)S(1)}, bf16[8,64,1280]{2,1,0:T(8,128)(2,1)}, u32[]{:S(2)}, u32[]{:S(2)}) collective-permute-start(bf16[8,64,1280]{2,1,0:T(8,128)(2,1)S(1)} %get-tuple-element.23), channel_id=1, source_target_pairs={{0,1},{1,0},{2,3},{3,2},{4,5},{5,4},{6,7},{7,6},{8,9},{9,8},{10,11... | collective-permute-start | bytes 3932168 | tf_op jit(solution)/shard_map/ppermute | solution.py:308
  108.5 18.3 %all-to-all-start.5 = ((bf16[64,4,256]{2,1,0:T(4,128)(2,1)}), bf16[64,4,256]{2,1,0:T(4,128)(2,1)S(1)}, u32[]{:S(2)}, u32[]{:S(2)}) async-start(bf16[64,4,256]{2,1,0:T(4,128)(2,1)} %get-tuple-element.17), calls=%async_computation.5 | async-start | bytes 262144 | tf_op jit(solution)/shard_map/all_to_all | solution.py:26
  126.8 30.8 %all-to-all-start.6 = ((bf16[8,64,1280]{2,1,0:T(8,128)(2,1)}), bf16[8,64,1280]{2,1,0:T(8,128)(2,1)S(1)}, u32[]{:S(2)}, u32[]{:S(2)}) async-start(bf16[8,64,1280]{2,1,0:T(8,128)(2,1)} %add_convert_fusion), calls=%async_computation.6 | async-start | bytes 2621440 | tf_op jit(solution)/shard_map/all_to_all | solution.py:26
  158.6 14.2 %all-to-all-start.7 = ((bf16[8,72,256]{2,1,0:T(8,128)(2,1)}), bf16[8,72,256]{2,1,0:T(8,128)(2,1)S(1)}, u32[]{:S(2)}, u32[]{:S(2)}) async-start(bf16[8,72,256]{2,1,0:T(8,128)(2,1)} %pad_maximum_fusion.1), calls=%async_computation.7 | async-start | bytes 589824 | tf_op jit(solution)/shard_map/all_to_all | solution.py:26
